TPU v7x, 32 devices: a whole 2x2x4 slice. The times are simulated.
32 devices in a mesh: ctx: 8 (over y, x, core), head: 4 (over z).
Axes of the slice: x: 2, y: 2, z: 4, core: 2. Of those that a mesh axis runs over, the one named last changes fastest.
Arguments:
- queries: bfloat16 [8192, 1024], P('ctx', 'head'), may hold values from -8 to 8
- keys: bfloat16 [8192, 256], P('ctx'), may hold values from -8 to 8
- values: bfloat16 [8192, 256], P('ctx'), may hold values from -8 to 8
- grad_out: bfloat16 [8192, 1024], P('ctx', 'head'), may hold values from -8 to 8
- block_index: int32 [8, 3], replicated, may hold values from 0 to 3
Outputs:
- grad_queries: bfloat16 [8192, 1024], P(('ctx', 'head'))
- grad_keys: bfloat16 [8192, 256], P(('ctx', 'head'))
- grad_values: bfloat16 [8192, 256], P(('ctx', 'head'))
Inputs may be any that keep to these rules, and one draw needn't show every extreme that they name: block_index[c, l] is read only where c >= 2**l.
All inputs are finite; a program needn't handle non-finite values.
Results may differ from a plain program's by a relative error of at most 0.023.
Values may be sent and summed in bfloat16 or wider, within the bound.
A program may use at most 64 MiB of HBM per device.

v0:
```python
import jax
import jax.numpy as jnp
from jax import lax
from jax.sharding import PartitionSpec as P

HD = 128
BLK = 256


def from_behind(value, axis, steps):
    count = lax.axis_size(axis)
    leading, last = (max(0, -steps), min(count, count - steps))
    return lax.ppermute(value, axis, [(source, source + steps) for source in range(leading, last)])


def attend(queries, grad_out, key_all, value_all, ctx_index, levels, local_heads):
    softmax_scale = HD ** (-0.5)
    shard_rows = queries.shape[0]
    key_count = key_all.shape[0]
    block_rows = min(512, shard_rows)
    partner_live = jnp.concatenate(
        [jnp.broadcast_to(ctx_index >= 2**level_num, (BLK,)) for level_num in range(levels)]
    )
    key_position = jnp.arange(shard_rows)
    key_acc = jnp.zeros((key_count, HD), jnp.float32)
    value_acc = jnp.zeros((key_count, HD), jnp.float32)
    dq_columns = []
    for head_slot in range(local_heads):
        query_head = queries[:, head_slot * HD : (head_slot + 1) * HD]
        grad_head = grad_out[:, head_slot * HD : (head_slot + 1) * HD]
        pieces = []
        for row_start in range(0, shard_rows, block_rows):
            query_rows = query_head[row_start : row_start + block_rows]
            grad_rows = grad_head[row_start : row_start + block_rows]
            causal_part = key_position[None, :] <= (row_start + jnp.arange(block_rows))[:, None]
            visible = jnp.concatenate(
                [causal_part, jnp.broadcast_to(partner_live[None, :], (block_rows, levels * BLK))],
                axis=1,
            )
            scores = (
                jnp.einsum("qd,kd->qk", query_rows, key_all, preferred_element_type=jnp.float32)
                * softmax_scale
            )
            scores = jnp.where(visible, scores, -jnp.inf)
            row_max = jnp.max(scores, axis=-1, keepdims=True)
            weights = jnp.exp(scores - row_max)
            probs = weights / jnp.sum(weights, axis=-1, keepdims=True)
            probs_low = probs.astype(jnp.bfloat16)
            grad_probs = jnp.einsum(
                "qd,kd->qk", grad_rows, value_all, preferred_element_type=jnp.float32
            )
            delta = jnp.sum(probs * grad_probs, axis=-1, keepdims=True)
            scores_low = (probs * (grad_probs - delta)).astype(jnp.bfloat16)
            pieces.append(
                (
                    softmax_scale * jnp.dot(scores_low, key_all, preferred_element_type=jnp.float32)
                ).astype(jnp.bfloat16)
            )
            key_acc = key_acc + softmax_scale * jnp.einsum(
                "qk,qd->kd", scores_low, query_rows, preferred_element_type=jnp.float32
            )
            value_acc = value_acc + jnp.einsum(
                "qk,qd->kd", probs_low, grad_rows, preferred_element_type=jnp.float32
            )
        dq_columns.append(jnp.concatenate(pieces, axis=0))
    return (jnp.concatenate(dq_columns, axis=1), key_acc, value_acc)


def on_device(queries, keys, values, grad_out, block_index):
    shard_rows = queries.shape[0]
    local_heads = queries.shape[1] // HD
    ctx_count = lax.axis_size("ctx")
    head_count = lax.axis_size("head")
    levels = ctx_count.bit_length() - 1
    ctx_index = lax.axis_index("ctx")
    head_index = lax.axis_index("head")
    group_begin = head_index // 2 * HD
    key_own = lax.dynamic_slice_in_dim(keys, group_begin, HD, 1)
    value_own = lax.dynamic_slice_in_dim(values, group_begin, HD, 1)
    kv_whole = jnp.concatenate([key_own, value_own], axis=1)

    def block_start(level_num):
        target = jnp.minimum(ctx_index + 2**level_num, ctx_count - 1)
        return block_index[target, level_num] * BLK

    received = []
    for level_num in range(levels):
        sliced = lax.dynamic_slice_in_dim(kv_whole, block_start(level_num), BLK, 0)
        received.append(from_behind(sliced, "ctx", 2**level_num))
    blocks = jnp.concatenate(received, axis=0)
    joined = jnp.concatenate([kv_whole, blocks], axis=0)
    key_all = joined[:, :HD]
    value_all = joined[:, HD:]
    dq_local, key_acc, value_acc = attend(
        queries, grad_out, key_all, value_all, ctx_index, levels, local_heads
    )
    gradients = jnp.concatenate([key_acc, value_acc], axis=1)
    owned = gradients[:shard_rows]
    for level_num in range(levels):
        lower = shard_rows + level_num * BLK
        returned = from_behind(
            gradients[lower : lower + BLK].astype(jnp.bfloat16), "ctx", -(2**level_num)
        ).astype(jnp.float32)
        begin = block_start(level_num)
        current = lax.dynamic_slice_in_dim(owned, begin, returned.shape[0], 0)
        owned = lax.dynamic_update_slice_in_dim(owned, current + returned, begin, 0)
    regrouped = lax.all_to_all(
        owned.astype(jnp.bfloat16), "head", split_axis=0, concat_axis=1, tiled=True
    ).astype(owned.dtype)
    token_rows = regrouped.shape[0]
    paired = regrouped.reshape(token_rows, head_count // 2, 2, 2 * HD)
    paired = paired[:, :, 0] + paired[:, :, 1]
    grad_keys = paired[:, :, :HD].reshape(token_rows, head_count // 2 * HD).astype(jnp.bfloat16)
    grad_values = paired[:, :, HD:].reshape(token_rows, head_count // 2 * HD).astype(jnp.bfloat16)
    grad_queries = lax.all_to_all(dq_local, "head", split_axis=0, concat_axis=1, tiled=True)
    return (grad_queries, grad_keys, grad_values)


def solution(mesh):
    placed = (P("ctx", "head"), P("ctx", None), P("ctx", None), P("ctx", "head"), P())
    return jax.shard_map(
        on_device,
        mesh=mesh,
        in_specs=placed,
        out_specs=(P(("ctx", "head"), None), P(("ctx", "head"), None), P(("ctx", "head"), None)),
        check_vma=False,
    )
```

profile of v0, /device:TPU:4, one launch (start us, length us, event | category | flops | bytes accessed | tf_op | source)
XLA Modules:
  0.0 81.1 jit_solution(12310010526575951676)
XLA Ops:
  0.7 1.4 %constant_dynamic-slice_fusion = (s32[1,1]{0,1:T(1,128)}, s32[1,1]{0,1:T(1,128)}, s32[1,1]{0,1:T(1,128)}) fusion(s32[8,3]{0,1:T(4,128)} %param.9, s32[]{:T(128)S(6)} %select_n.51, s32[]{:T(128)S(6)} %select_n.55, s32[]{:T(128)S(6)} %select_n.53), kind=kLoop, calls=%fused_computation.117 | loop fusion | bytes 36 | tf_op jit(solution)/shard_map/dynamic_slice | solution.py:84
  4.0 1.1 %constant_dynamic-slice_fusion.1 = (bf16[1024,128]{1,0:T(8,128)(2,1)S(1)}, bf16[1024,128]{1,0:T(8,128)(2,1)S(1)}) fusion(bf16[1024,256]{1,0:T(8,128)(2,1)} %param.7, s32[]{:T(128)S(6)} %select_n.50, bf16[1024,256]{1,0:T(8,128)(2,1)} %param.6), kind=kLoop, calls=%fused_computation.118 | loop fusion | bytes 1048580 | tf_op jit(solution)/shard_map/dynamic_slice | solution.py:79
  5.2 1.9 %collective-permute-start = (bf16[256,256]{1,0:T(8,128)(2,1)S(1)}, bf16[256,256]{1,0:T(8,128)(2,1)S(1)}, u32[]{:S(2)}, u32[]{:S(2)}) collective-permute-start(bf16[256,256]{1,0:T(8,128)(2,1)S(1)} %get-tuple-element.6), channel_id=1, source_target_pairs={{0,4},{4,8},{8,12},{12,16},{16,20},{20,24},{24,28},{1,5},{5,9},{9,... | collective-permute-start | bytes 393224 | tf_op jit(solution)/shard_map/ppermute | solution.py:13
  7.1 3.4 %collective-permute-start.1 = (bf16[256,256]{1,0:T(8,128)(2,1)S(1)}, bf16[256,256]{1,0:T(8,128)(2,1)S(1)}, u32[]{:S(2)}, u32[]{:S(2)}) collective-permute-start(bf16[256,256]{1,0:T(8,128)(2,1)S(1)} %get-tuple-element.7), channel_id=1, source_target_pairs={{0,8},{4,12},{8,16},{12,20},{16,24},{20,28},{1,9},{5,13},{9,17},{1... | collective-permute-start | bytes 393224 | tf_op jit(solution)/shard_map/ppermute | solution.py:13
  10.5 1.3 %collective-permute-start.2 = (bf16[256,256]{1,0:T(8,128)(2,1)S(1)}, bf16[256,256]{1,0:T(8,128)(2,1)S(1)}, u32[]{:S(2)}, u32[]{:S(2)}) collective-permute-start(bf16[256,256]{1,0:T(8,128)(2,1)S(1)} %get-tuple-element.8), channel_id=1, source_target_pairs={{0,16},{4,20},{8,24},{12,28},{1,17},{5,21},{9,25},{13,29},{2,18},{... | collective-permute-start | bytes 393224 | tf_op jit(solution)/shard_map/ppermute | solution.py:13
  12.4 3.3 %collective-permute-done.1 = bf16[256,256]{1,0:T(8,128)(2,1)S(1)} collective-permute-done((bf16[256,256]{1,0:T(8,128)(2,1)S(1)}, bf16[256,256]{1,0:T(8,128)(2,1)S(1)}, u32[]{:S(2)}, u32[]{:S(2)}) %collective-permute-start.1) | collective-permute-done | bytes 131104 | tf_op jit(solution)/shard_map/ppermute | solution.py:13
  15.8 3.3 %collective-permute-done.2 = bf16[256,256]{1,0:T(8,128)(2,1)S(1)} collective-permute-done((bf16[256,256]{1,0:T(8,128)(2,1)S(1)}, bf16[256,256]{1,0:T(8,128)(2,1)S(1)}, u32[]{:S(2)}, u32[]{:S(2)}) %collective-permute-start.2) | collective-permute-done | bytes 131104 | tf_op jit(solution)/shard_map/ppermute | solution.py:13
  19.2 0.8 fusion.77
  20.0 0.8 fusion.79
  20.8 0.6 fusion.13
  21.3 0.8 %fusion.25 = f32[1792,128]{0,1:T(8,128)S(1)} fusion(bf16[1024,256]{1,0:T(8,128)(2,1)S(1)} %copy-done.1, f32[512,1792]{0,1:T(8,128)S(1)} %get-tuple-element.27, f32[512]{0:T(512)S(1)} %fusion.13, f32[512]{0:T(512)S(1)} %get-tuple-element.26), kind=kOutput, calls=%fused_computation.54 | convolution fusion | flops 237633536 | bytes 4722688 | tf_op jit(solution)/shard_map/qk,qd->kd/dot_general | solution.py:62
  22.2 0.8 %fusion.9 = (f32[512]{0:T(512)S(1)}, f32[1792,512]{1,0:T(8,128)S(1)}) fusion(f32[512]{0:T(512)S(1)} %fusion.13, f32[512,1792]{0,1:T(8,128)S(1)} %get-tuple-element.27, f32[512]{0:T(512)S(1)} %get-tuple-element.26, bf16[1024,256]{1,0:T(8,128)(2,1)S(1)} %copy-done.1, bf16[1792,256]{1,0:T(8,128)(2,1)S(1)} %pad_maximum_fusion.1), kind=kOutput, calls=%fused_computation.20 | convolution fusion | flops 238550528 | bytes 7936000 | tf_op jit(solution)/shard_map/qd,kd->qk/dot_general | solution.py:49
  23.0 1.0 %fusion.11 = bf16[512,1792]{0,1:T(8,128)(2,1)S(1)} fusion(f32[1792,512]{1,0:T(8,128)S(1)} %get-tuple-element.29, f32[512]{0:T(512)S(1)} %get-tuple-element.28, f32[512]{0:T(512)S(1)} %fusion.13, f32[512,1792]{0,1:T(8,128)S(1)} %get-tuple-element.27, f32[512]{0:T(512)S(1)} %get-tuple-element.26), kind=kLoop, calls=%fused_computation.22 | loop fusion | flops 4587520 | bytes 9181184 | tf_op jit(solution)/shard_map/convert_element_type | solution.py:53
  24.1 0.7 fusion.27
  24.8 0.7 fusion.59
  25.5 0.8 fusion.78
  26.3 0.8 fusion.76
  27.1 0.6 fusion.17
  27.6 0.9 %fusion.3 = (f32[512]{0:T(512)S(1)}, f32[1792,512]{1,0:T(8,128)S(1)}) fusion(f32[512]{0:T(512)S(1)} %fusion.17, f32[512,1792]{0,1:T(8,128)S(1)} %get-tuple-element.19, f32[512]{0:T(512)S(1)} %get-tuple-element.18, bf16[1024,256]{1,0:T(8,128)(2,1)S(1)} %copy-done.1, bf16[1792,256]{1,0:T(8,128)(2,1)S(1)} %pad_maximum_fusion.1), kind=kOutput, calls=%fused_computation.8 | convolution fusion | flops 238550528 | bytes 7936000 | tf_op jit(solution)/shard_map/qd,kd->qk/dot_general | solution.py:49
  28.5 1.0 %fusion.5 = bf16[512,1792]{0,1:T(8,128)(2,1)S(1)} fusion(f32[1792,512]{1,0:T(8,128)S(1)} %get-tuple-element.21, f32[512]{0:T(512)S(1)} %get-tuple-element.20, f32[512]{0:T(512)S(1)} %fusion.17, f32[512,1792]{0,1:T(8,128)S(1)} %get-tuple-element.19, f32[512]{0:T(512)S(1)} %get-tuple-element.18), kind=kLoop, calls=%fused_computation.10 | loop fusion | flops 4587520 | bytes 9181184 | tf_op jit(solution)/shard_map/convert_element_type | solution.py:53
  29.5 0.7 fusion.29
  30.2 0.6 fusion.15
  30.8 1.0 %fusion.6 = (f32[512]{0:T(512)S(1)}, f32[1792,512]{1,0:T(8,128)S(1)}) fusion(f32[512]{0:T(512)S(1)} %fusion.15, f32[512,1792]{0,1:T(8,128)S(1)} %get-tuple-element.23, f32[512]{0:T(512)S(1)} %get-tuple-element.22, bf16[1024,256]{1,0:T(8,128)(2,1)S(1)} %copy-done.1, bf16[1792,256]{1,0:T(8,128)(2,1)S(1)} %pad_maximum_fusion.1), kind=kOutput, calls=%fused_computation.14 | convolution fusion | flops 238550528 | bytes 7936000 | tf_op jit(solution)/shard_map/qd,kd->qk/dot_general | solution.py:49
  31.8 0.9 %convolution_add_fusion.2 = f32[1792,128]{0,1:T(8,128)S(1)} fusion(f32[1792,128]{0,1:T(8,128)S(1)} %fusion.25, bf16[1024,256]{1,0:T(8,128)(2,1)S(1)} %copy-done.1, f32[512,1792]{0,1:T(8,128)S(1)} %get-tuple-element.23, f32[512]{0:T(512)S(1)} %fusion.15, f32[512]{0:T(512)S(1)} %get-tuple-element.22), kind=kOutput, calls=%fused_computation.40 | convolution fusion | flops 237862912 | bytes 5640192 | tf_op jit(solution)/shard_map/qk,qd->kd/dot_general | solution.py:62
  32.7 0.9 %convolution_add_fusion.1 = f32[1792,128]{0,1:T(8,128)S(1)} fusion(f32[1792,128]{0,1:T(8,128)S(1)} %convolution_add_fusion.2, bf16[1024,256]{1,0:T(8,128)(2,1)S(1)} %copy-done.1, f32[512,1792]{0,1:T(8,128)S(1)} %get-tuple-element.19, f32[512]{0:T(512)S(1)} %fusion.17, f32[512]{0:T(512)S(1)} %get-tuple-element.18), kind=kOutput, calls=%fused_computation.39 | convolution fusion | flops 237862912 | bytes 5640192 | tf_op jit(solution)/shard_map/qk,qd->kd/dot_general | solution.py:62
  33.5 0.6 fusion.19
  34.1 0.8 %fusion = (f32[512]{0:T(512)S(1)}, f32[1792,512]{1,0:T(8,128)S(1)}) fusion(f32[512]{0:T(512)S(1)} %fusion.19, f32[512,1792]{0,1:T(8,128)S(1)} %get-tuple-element.15, f32[512]{0:T(512)S(1)} %get-tuple-element.14, bf16[1024,256]{1,0:T(8,128)(2,1)S(1)} %copy-done.1, bf16[1792,256]{1,0:T(8,128)(2,1)S(1)} %pad_maximum_fusion.1), kind=kOutput, calls=%fused_computation.2 | convolution fusion | flops 238550528 | bytes 7936000 | tf_op jit(solution)/shard_map/qd,kd->qk/dot_general | solution.py:49
  35.0 0.9 %convolution_add_fusion = f32[1792,128]{0,1:T(8,128)S(1)} fusion(f32[1792,128]{0,1:T(8,128)S(1)} %convolution_add_fusion.1, bf16[1024,256]{1,0:T(8,128)(2,1)S(1)} %copy-done.1, f32[512,1792]{0,1:T(8,128)S(1)} %get-tuple-element.15, f32[512]{0:T(512)S(1)} %fusion.19, f32[512]{0:T(512)S(1)} %get-tuple-element.14), kind=kOutput, calls=%fused_computation.38 | convolution fusion | flops 237862912 | bytes 5640192 | tf_op jit(solution)/shard_map/qk,qd->kd/dot_general | solution.py:62
  35.8 1.0 %fusion.2 = bf16[512,1792]{0,1:T(8,128)(2,1)S(1)} fusion(f32[1792,512]{1,0:T(8,128)S(1)} %get-tuple-element.17, f32[512]{0:T(512)S(1)} %get-tuple-element.16, f32[512]{0:T(512)S(1)} %fusion.19, f32[512,1792]{0,1:T(8,128)S(1)} %get-tuple-element.15, f32[512]{0:T(512)S(1)} %get-tuple-element.14), kind=kLoop, calls=%fused_computation.4 | loop fusion | flops 4587520 | bytes 9181184 | tf_op jit(solution)/shard_map/convert_element_type | solution.py:53
  36.9 0.7 fusion.30
  37.6 1.0 %fusion.8 = bf16[512,1792]{0,1:T(8,128)(2,1)S(1)} fusion(f32[1792,512]{1,0:T(8,128)S(1)} %get-tuple-element.25, f32[512]{0:T(512)S(1)} %get-tuple-element.24, f32[512]{0:T(512)S(1)} %fusion.15, f32[512,1792]{0,1:T(8,128)S(1)} %get-tuple-element.23, f32[512]{0:T(512)S(1)} %get-tuple-element.22), kind=kLoop, calls=%fused_computation.16 | loop fusion | flops 4587520 | bytes 9181184 | tf_op jit(solution)/shard_map/convert_element_type | solution.py:53
  38.6 0.7 fusion.28
  39.3 0.7 convolution_add_fusion.5
  40.0 0.7 convolution_add_fusion.4
  40.8 0.7 fusion.20
  41.5 0.9 %maximum_maximum_fusion = bf16[1024,256]{1,0:T(8,128)(2,1)} fusion(bf16[512,128]{1,0:T(8,128)(2,1)S(1)} %fusion.30, bf16[512,128]{1,0:T(8,128)(2,1)S(1)} %fusion.29, bf16[512,128]{1,0:T(8,128)(2,1)S(1)} %fusion.28, bf16[512,128]{1,0:T(8,128)(2,1)S(1)} %fusion.27), kind=kLoop, calls=%fused_computation.75 | loop fusion | flops 2097152 | bytes 1048576 | tf_op jit(solution)/shard_map/concatenate | solution.py:66
  42.4 4.9 %all-to-all-start = ((bf16[4,256,256]{2,1,0:T(8,128)(2,1)}), bf16[4,256,256]{2,1,0:T(8,128)(2,1)S(1)}, u32[]{:S(2)}, u32[]{:S(2)}) async-start(bf16[4,256,256]{2,1,0:T(8,128)(2,1)} %bitcast.11), calls=%async_computation | async-start | bytes 1048576 | tf_op jit(solution)/shard_map/all_to_all | solution.py:115
  47.4 1.5 %collective-permute-start.5 = (bf16[256,256]{0,1:T(8,128)(2,1)S(1)}, bf16[256,256]{0,1:T(8,128)(2,1)S(1)}, u32[]{:S(2)}, u32[]{:S(2)}) collective-permute-start(bf16[256,256]{0,1:T(8,128)(2,1)S(1)} %get-tuple-element.3), channel_id=1, source_target_pairs={{16,0},{20,4},{24,8},{28,12},{17,1},{21,5},{25,9},{29,13},{18,2},{... | collective-permute-start | bytes 393224 | tf_op jit(solution)/shard_map/ppermute | solution.py:13
  48.8 1.9 %collective-permute-start.4 = (bf16[256,256]{0,1:T(8,128)(2,1)S(1)}, bf16[256,256]{0,1:T(8,128)(2,1)S(1)}, u32[]{:S(2)}, u32[]{:S(2)}) collective-permute-start(bf16[256,256]{0,1:T(8,128)(2,1)S(1)} %get-tuple-element.4), channel_id=1, source_target_pairs={{8,0},{12,4},{16,8},{20,12},{24,16},{28,20},{9,1},{13,5},{17,9},{2... | collective-permute-start | bytes 393224 | tf_op jit(solution)/shard_map/ppermute | solution.py:13
  50.8 1.9 %collective-permute-start.3 = (bf16[256,256]{0,1:T(8,128)(2,1)S(1)}, bf16[256,256]{0,1:T(8,128)(2,1)S(1)}, u32[]{:S(2)}, u32[]{:S(2)}) collective-permute-start(bf16[256,256]{0,1:T(8,128)(2,1)S(1)} %get-tuple-element.5), channel_id=1, source_target_pairs={{4,0},{8,4},{12,8},{16,12},{20,16},{24,20},{28,24},{5,1},{9,5},{13... | collective-permute-start | bytes 393224 | tf_op jit(solution)/shard_map/ppermute | solution.py:13
  52.8 2.4 %collective-permute-done.3 = bf16[256,256]{0,1:T(8,128)(2,1)S(1)} collective-permute-done((bf16[256,256]{0,1:T(8,128)(2,1)S(1)}, bf16[256,256]{0,1:T(8,128)(2,1)S(1)}, u32[]{:S(2)}, u32[]{:S(2)}) %collective-permute-start.3) | collective-permute-done | bytes 131104 | tf_op jit(solution)/shard_map/ppermute | solution.py:13
  55.9 0.8 %copy.20 = bf16[32,4,8,256]{3,2,0,1:T(8,128)(2,1)} copy(bf16[32,4,8,256]{3,2,1,0:T(8,128)(2,1)S(1)} %bitcast.71) | data formatting | bytes 1048576 | tf_op jit(solution)/shard_map/all_to_all | solution.py:107
  56.8 5.2 %all-to-all-done = bf16[4,256,256]{2,1,0:T(8,128)(2,1)S(1)} async-done(((bf16[4,256,256]{2,1,0:T(8,128)(2,1)}), bf16[4,256,256]{2,1,0:T(8,128)(2,1)S(1)}, u32[]{:S(2)}, u32[]{:S(2)}) %all-to-all-start) | async-done | bytes 524320 | tf_op jit(solution)/shard_map/all_to_all | solution.py:115
  61.9 3.5 %all-to-all-start.1 = ((bf16[4,256,256]{1,2,0:T(8,128)(2,1)}), bf16[4,256,256]{1,2,0:T(8,128)(2,1)S(1)}, u32[]{:S(2)}, u32[]{:S(2)}) async-start(bf16[4,256,256]{1,2,0:T(8,128)(2,1)} %bitcast.69), calls=%async_computation.1 | async-start | bytes 1048576 | tf_op jit(solution)/shard_map/all_to_all | solution.py:107
  65.4 0.9 %copy.18 = bf16[4,32,8,256]{3,2,0,1:T(8,128)(2,1)} copy(bf16[4,32,8,256]{3,2,1,0:T(8,128)(2,1)S(1)} %bitcast.72) | data formatting | bytes 1048576 | tf_op jit(solution)/shard_map/all_to_all | solution.py:115
  66.3 13.1 %all-to-all-done.1 = bf16[4,256,256]{1,2,0:T(8,128)(2,1)S(1)} async-done(((bf16[4,256,256]{1,2,0:T(8,128)(2,1)}), bf16[4,256,256]{1,2,0:T(8,128)(2,1)S(1)}, u32[]{:S(2)}, u32[]{:S(2)}) %all-to-all-start.1) | async-done | bytes 524320 | tf_op jit(solution)/shard_map/all_to_all | solution.py:107
  79.6 0.8 copy.16
  80.3 0.8 copy.15
  (27 shorter events, 1.9 us)
Async XLA Ops:
  0.6 18.5 %copy-start = (bf16[1024,256]{1,0:T(8,128)(2,1)S(1)}, bf16[1024,256]{1,0:T(8,128)(2,1)}, u32[]{:S(2)}) copy-start(bf16[1024,256]{1,0:T(8,128)(2,1)} %param.5) | copy-start | bytes 1572868
  5.2 7.3 %collective-permute-start = (bf16[256,256]{1,0:T(8,128)(2,1)S(1)}, bf16[256,256]{1,0:T(8,128)(2,1)S(1)}, u32[]{:S(2)}, u32[]{:S(2)}) collective-permute-start(bf16[256,256]{1,0:T(8,128)(2,1)S(1)} %get-tuple-element.6), channel_id=1, source_target_pairs={{0,4},{4,8},{8,12},{12,16},{16,20},{20,24},{24,28},{1,5},{5,9},{9,... | collective-permute-start | bytes 393224 | tf_op jit(solution)/shard_map/ppermute | solution.py:13
  7.1 8.7 %collective-permute-start.1 = (bf16[256,256]{1,0:T(8,128)(2,1)S(1)}, bf16[256,256]{1,0:T(8,128)(2,1)S(1)}, u32[]{:S(2)}, u32[]{:S(2)}) collective-permute-start(bf16[256,256]{1,0:T(8,128)(2,1)S(1)} %get-tuple-element.7), channel_id=1, source_target_pairs={{0,8},{4,12},{8,16},{12,20},{16,24},{20,28},{1,9},{5,13},{9,17},{1... | collective-permute-start | bytes 393224 | tf_op jit(solution)/shard_map/ppermute | solution.py:13
  10.5 8.6 %collective-permute-start.2 = (bf16[256,256]{1,0:T(8,128)(2,1)S(1)}, bf16[256,256]{1,0:T(8,128)(2,1)S(1)}, u32[]{:S(2)}, u32[]{:S(2)}) collective-permute-start(bf16[256,256]{1,0:T(8,128)(2,1)S(1)} %get-tuple-element.8), channel_id=1, source_target_pairs={{0,16},{4,20},{8,24},{12,28},{1,17},{5,21},{9,25},{13,29},{2,18},{... | collective-permute-start | bytes 393224 | tf_op jit(solution)/shard_map/ppermute | solution.py:13
  20.0 1.4 %copy-start.1 = (bf16[1024,256]{1,0:T(8,128)(2,1)S(1)}, bf16[1024,256]{1,0:T(8,128)(2,1)}, u32[]{:S(2)}) copy-start(bf16[1024,256]{1,0:T(8,128)(2,1)} %param.8) | copy-start | bytes 1572868
  42.4 19.6 %all-to-all-start = ((bf16[4,256,256]{2,1,0:T(8,128)(2,1)}), bf16[4,256,256]{2,1,0:T(8,128)(2,1)S(1)}, u32[]{:S(2)}, u32[]{:S(2)}) async-start(bf16[4,256,256]{2,1,0:T(8,128)(2,1)} %bitcast.11), calls=%async_computation | async-start | bytes 1048576 | tf_op jit(solution)/shard_map/all_to_all | solution.py:115
  47.4 8.4 %collective-permute-start.5 = (bf16[256,256]{0,1:T(8,128)(2,1)S(1)}, bf16[256,256]{0,1:T(8,128)(2,1)S(1)}, u32[]{:S(2)}, u32[]{:S(2)}) collective-permute-start(bf16[256,256]{0,1:T(8,128)(2,1)S(1)} %get-tuple-element.3), channel_id=1, source_target_pairs={{16,0},{20,4},{24,8},{28,12},{17,1},{21,5},{25,9},{29,13},{18,2},{... | collective-permute-start | bytes 393224 | tf_op jit(solution)/shard_map/ppermute | solution.py:13
  48.8 6.9 %collective-permute-start.4 = (bf16[256,256]{0,1:T(8,128)(2,1)S(1)}, bf16[256,256]{0,1:T(8,128)(2,1)S(1)}, u32[]{:S(2)}, u32[]{:S(2)}) collective-permute-start(bf16[256,256]{0,1:T(8,128)(2,1)S(1)} %get-tuple-element.4), channel_id=1, source_target_pairs={{8,0},{12,4},{16,8},{20,12},{24,16},{28,20},{9,1},{13,5},{17,9},{2... | collective-permute-start | bytes 393224 | tf_op jit(solution)/shard_map/ppermute | solution.py:13
  50.8 4.4 %collective-permute-start.3 = (bf16[256,256]{0,1:T(8,128)(2,1)S(1)}, bf16[256,256]{0,1:T(8,128)(2,1)S(1)}, u32[]{:S(2)}, u32[]{:S(2)}) collective-permute-start(bf16[256,256]{0,1:T(8,128)(2,1)S(1)} %get-tuple-element.5), channel_id=1, source_target_pairs={{4,0},{8,4},{12,8},{16,12},{20,16},{24,20},{28,24},{5,1},{9,5},{13... | collective-permute-start | bytes 393224 | tf_op jit(solution)/shard_map/ppermute | solution.py:13
  61.9 17.5 %all-to-all-start.1 = ((bf16[4,256,256]{1,2,0:T(8,128)(2,1)}), bf16[4,256,256]{1,2,0:T(8,128)(2,1)S(1)}, u32[]{:S(2)}, u32[]{:S(2)}) async-start(bf16[4,256,256]{1,2,0:T(8,128)(2,1)} %bitcast.69), calls=%async_computation.1 | async-start | bytes 1048576 | tf_op jit(solution)/shard_map/all_to_all | solution.py:107
where the time goes:
time: 82 us; the launch traced here: 81.1 us
  waiting for transfers between devices  27.8 us (34%)
  starting transfers between devices  20.2 us (25%)
  matrix products  15.8 us (19%)
  other arithmetic  8.57 us (10%)
  local copies, waits for them, and re-layouts  5.75 us (7%)
  between operations  2.98 us (4%)
    all_to_all x1, waiting for transfers between devices, on_device(): lax.all_to_all(owned.astype(jnp.bfloat16), 'head', split_axis=0, concat_a...  13.1 us
    ppermute x6, starting transfers between devices, from_behind(): lax.ppermute(value, axis, [(source, source + steps) for source in range(l...  11.9 us
    ppermute x6, waiting for transfers between devices, from_behind(): lax.ppermute(value, axis, [(source, source + steps) for source in range(l...  9.47 us
    all_to_all x1, waiting for transfers between devices, on_device(): lax.all_to_all(dq_local, 'head', split_axis=0, concat_axis=1, tiled=True)  5.16 us
    all_to_all x1, starting transfers between devices, on_device(): lax.all_to_all(dq_local, 'head', split_axis=0, concat_axis=1, tiled=True)  4.87 us
    convert_element_type x4, other arithmetic, attend(): scores_low = (probs * (grad_probs - delta)).astype(jnp.bfloat16)  4.17 us
    dot_general x4, matrix products, attend(): jnp.einsum('qd,kd->qk', grad_rows, value_all, preferred_element_type=jnp....  3.57 us
    all_to_all x1, starting transfers between devices, on_device(): lax.all_to_all(owned.astype(jnp.bfloat16), 'head', split_axis=0, concat_a...  3.47 us
  transfers between devices with their start and end apart: 8, of which 6 were waited for; matrix products, arithmetic and copies ran while one was open for 3% of the time, Pallas kernels for 0%

commit v1 on v0

v1 whole, which is shorter than its diff:
```python
import functools

import jax
import jax.numpy as jnp
from jax import lax
from jax.experimental import pallas as pl
from jax.experimental.pallas import tpu as pltpu
from jax.sharding import PartitionSpec as P

HD = 128
BLK = 256
LOG2E = 1.4426950408889634
MESH = pl.DeviceIdType.MESH
NT = (((1,), (1,)), ((), ()))
NN = (((1,), (0,)), ((), ()))


def dot(a, b, dims=NN):
    return lax.dot_general(a, b, dims, preferred_element_type=jnp.float32)


def kernel(
    sizes,
    q_ref,
    do_ref,
    k_ref,
    v_ref,
    index_ref,
    dq_out,
    gk_out,
    gv_out,
    own_kv,
    own_kt,
    part_kt,
    kv_send,
    kv_recv,
    w_own,
    dp_own,
    w_part,
    dp_part,
    dq_part,
    acc,
    acc_part,
    ret_send,
    ret_recv,
    dq_stage,
    pair_send,
    pair_recv,
    final,
    kv_ssem,
    kv_rsem,
    ret_ssem,
    ret_rsem,
    dq_ssem,
    dq_rsem,
    pair_ssem,
    pair_rsem,
    fin_ssem,
    fin_rsem,
):
    n_ctx, n_head, kv_heads, local_heads, shard_rows, levels = sizes
    repl = n_head // kv_heads
    per_member = n_head // repl
    rows_out = shard_rows // n_head
    tiles = shard_rows // BLK
    cols = local_heads * BLK
    width = local_heads * HD
    scale = HD ** (-0.5)
    c2 = scale * LOG2E
    ctx = lax.axis_index("ctx")
    head = lax.axis_index("head")
    group = head // repl
    member = head % repl
    gcol = pl.multiple_of(group * HD, HD)

    barrier = pltpu.get_barrier_semaphore()
    greet = n_head - 1
    for level in range(levels):
        step = 2**level

        @pl.when(ctx + step < n_ctx)
        def _():
            pl.semaphore_signal(barrier, inc=1, device_id=(ctx + step, head), device_id_type=MESH)

        @pl.when(ctx >= step)
        def _():
            pl.semaphore_signal(barrier, inc=1, device_id=(ctx - step, head), device_id_type=MESH)

        greet = greet + jnp.where(ctx + step < n_ctx, 1, 0) + jnp.where(ctx >= step, 1, 0)
    for off in range(1, n_head):
        pl.semaphore_signal(
            barrier, inc=1, device_id=(ctx, (head + off) % n_head), device_id_type=MESH
        )

    own_kv[:, :HD] = k_ref[:, pl.ds(gcol, HD)]
    own_kv[:, HD:] = v_ref[:, pl.ds(gcol, HD)]
    blocks = []

    def is_block(level, block):
        return (blocks[level] == block).astype(jnp.float32)

    for level in range(levels):
        target = jnp.minimum(ctx + 2**level, n_ctx - 1)
        blocks.append(index_ref[target, level])
        chosen = jnp.zeros((BLK, 2 * HD), jnp.float32)
        for block in range(tiles):
            piece = own_kv[block * BLK : (block + 1) * BLK, :].astype(jnp.float32)
            chosen = chosen + piece * is_block(level, block)
        kv_send[level] = chosen.astype(jnp.bfloat16)

    pl.semaphore_wait(barrier, greet)

    def kv_copy(level):
        return pltpu.make_async_remote_copy(
            src_ref=kv_send.at[level],
            dst_ref=kv_recv.at[level],
            send_sem=kv_ssem.at[level],
            recv_sem=kv_rsem.at[level],
            device_id=(jnp.minimum(ctx + 2**level, n_ctx - 1), head),
            device_id_type=MESH,
        )

    for level in reversed(range(levels)):

        @pl.when(ctx + 2**level < n_ctx)
        def _():
            kv_copy(level).start()

        @pl.when(ctx < 2**level)
        def _():
            kv_recv[level] = jnp.zeros((BLK, 2 * HD), jnp.bfloat16)

        @pl.when(ctx + 2**level >= n_ctx)
        def _():
            ret_recv[level] = jnp.zeros((BLK, 2 * HD), jnp.bfloat16)

    def stacked(ref, tile):
        rows = pl.ds(tile * BLK, BLK)
        return jnp.concatenate(
            [ref[rows, h * HD : (h + 1) * HD] for h in range(local_heads)], axis=0
        )

    def slot(tile, block):
        return tile * (tile + 1) // 2 + block

    order = list(reversed(range(tiles)))
    key_pos = lax.broadcasted_iota(jnp.int32, (BLK, cols), 0)
    query_pos = lax.broadcasted_iota(jnp.int32, (BLK, cols), 1) % BLK
    for block in range(tiles):
        rows = pl.ds(block * BLK, BLK)
        own_kt[:, rows] = own_kv[rows, :HD].T

    own_stats = {}
    for tile in order:
        q_cat, do_cat = stacked(q_ref, tile), stacked(do_ref, tile)
        top = None
        for block in range(tile + 1):
            s = dot(own_kv[block * BLK : (block + 1) * BLK, :HD], q_cat, NT)
            if block == tile:
                s = jnp.where(key_pos <= query_pos, s, -1e30)
            w_own[slot(tile, block)] = s
            high = jnp.max(s, axis=0, keepdims=True)
            top = high if top is None else jnp.maximum(top, high)
        top = top * c2
        total = jnp.zeros((1, cols), jnp.float32)
        mixed = jnp.zeros((1, cols), jnp.float32)
        for block in range(tile + 1):
            w = jnp.exp2(w_own[slot(tile, block)] * c2 - top)
            dp = dot(own_kv[block * BLK : (block + 1) * BLK, HD:], do_cat, NT)
            w_own[slot(tile, block)] = w
            dp_own[slot(tile, block)] = dp
            total = total + jnp.sum(w, axis=0, keepdims=True)
            mixed = mixed + jnp.sum(w * dp, axis=0, keepdims=True)
        own_stats[tile] = (top, total, mixed)

    for level in range(levels):

        @pl.when(ctx >= 2**level)
        def _():
            kv_copy(level).wait_recv()

    dead = []
    for level in range(levels):
        part_kt[:, level * BLK : (level + 1) * BLK] = kv_recv[level, :, :HD].T
        dead.append(jnp.where(ctx >= 2**level, 0.0, 1e30).astype(jnp.float32))

    final_stats = {}
    for tile in order:
        q_cat, do_cat = stacked(q_ref, tile), stacked(do_ref, tile)
        top_own, total_own, mixed_own = own_stats[tile]
        top = top_own
        for level in range(levels):
            s = dot(kv_recv[level, :, :HD], q_cat, NT)
            w_part[level] = s
            top = jnp.maximum(top, jnp.max(s, axis=0, keepdims=True) * c2 - dead[level])
        keep = jnp.exp2(top_own - top)
        total = total_own * keep
        mixed = mixed_own * keep
        for level in range(levels):
            w = jnp.exp2(w_part[level] * c2 - (top + dead[level]))
            dp = dot(kv_recv[level, :, HD:], do_cat, NT)
            w_part[level] = w
            dp_part[level] = dp
            total = total + jnp.sum(w, axis=0, keepdims=True)
            mixed = mixed + jnp.sum(w * dp, axis=0, keepdims=True)
        inverse = 1.0 / total
        delta = mixed * inverse
        final_stats[tile] = (keep * inverse, delta)
        dq_t = None
        for level in range(levels):
            p = w_part[level] * inverse
            ds = (p * (dp_part[level] - delta)).astype(jnp.bfloat16)
            d_value = dot(p.astype(jnp.bfloat16), do_cat)
            d_key = dot(ds, q_cat) * scale
            if tile == order[0]:
                acc_part[level, :, :HD] = d_key
                acc_part[level, :, HD:] = d_value
            else:
                acc_part[level, :, :HD] += d_key
                acc_part[level, :, HD:] += d_value
            piece = dot(part_kt[:, level * BLK : (level + 1) * BLK], ds)
            dq_t = piece if dq_t is None else dq_t + piece
        dq_part[tile] = dq_t

    def ret_copy(level):
        return pltpu.make_async_remote_copy(
            src_ref=ret_send.at[level],
            dst_ref=ret_recv.at[level],
            send_sem=ret_ssem.at[level],
            recv_sem=ret_rsem.at[level],
            device_id=(jnp.maximum(ctx - 2**level, 0), head),
            device_id_type=MESH,
        )

    for level in reversed(range(levels)):
        ret_send[level] = acc_part[level].astype(jnp.bfloat16)

        @pl.when(ctx >= 2**level)
        def _():
            ret_copy(level).start()

    def dq_copy(dest, source):
        return pltpu.make_async_remote_copy(
            src_ref=dq_stage.at[pl.ds(dest * rows_out, rows_out), :],
            dst_ref=dq_out.at[:, pl.ds(pl.multiple_of(source * width, width), width)],
            send_sem=dq_ssem.at[dest],
            recv_sem=dq_rsem.at[source],
            device_id=(ctx, dest),
            device_id_type=MESH,
        )

    for tile in order:
        q_cat, do_cat = stacked(q_ref, tile), stacked(do_ref, tile)
        inverse, delta = final_stats[tile]
        dq_t = dq_part[tile]
        for block in range(tile + 1):
            p = w_own[slot(tile, block)] * inverse
            ds = (p * (dp_own[slot(tile, block)] - delta)).astype(jnp.bfloat16)
            d_value = dot(p.astype(jnp.bfloat16), do_cat)
            d_key = dot(ds, q_cat) * scale
            rows = slice(block * BLK, (block + 1) * BLK)
            if tile == order[0]:
                acc[rows, :HD] = d_key
                acc[rows, HD:] = d_value
            else:
                acc[rows, :HD] += d_key
                acc[rows, HD:] += d_value
            dq_t = dq_t + dot(own_kt[:, rows], ds)
        dq_t = dq_t * scale
        for h in range(local_heads):
            dq_stage[tile * BLK : (tile + 1) * BLK, h * HD : (h + 1) * HD] = (
                dq_t[:, h * BLK : (h + 1) * BLK].T.astype(jnp.bfloat16)
            )
        for dest in range(tile * BLK // rows_out, (tile + 1) * BLK // rows_out):

            @pl.when(head != dest)
            def _():
                dq_copy(dest, head).start()

            @pl.when(head == dest)
            def _():
                dq_out[:, pl.ds(pl.multiple_of(head * width, width), width)] = dq_stage[
                    dest * rows_out : (dest + 1) * rows_out, :
                ]

    for level in range(levels):

        @pl.when(ctx + 2**level < n_ctx)
        def _():
            ret_copy(level).wait_recv()

    for block in range(tiles):
        rows = slice(block * BLK, (block + 1) * BLK)
        value = acc[rows, :]
        for level in range(levels):
            back = ret_recv[level].astype(jnp.float32)
            value = value + back * is_block(level, block)
        acc[rows, :] = value

    def pair_copy(off, k):
        return pltpu.make_async_remote_copy(
            src_ref=pair_send.at[off - 1, k],
            dst_ref=pair_recv.at[off - 1, k],
            send_sem=pair_ssem.at[off - 1, k],
            recv_sem=pair_rsem.at[off - 1, k],
            device_id=(ctx, group * repl + (member + off) % repl),
            device_id_type=MESH,
        )

    for k in range(per_member):
        for off in range(1, repl):
            begin = pl.multiple_of((k * repl + (member + off) % repl) * rows_out, rows_out)
            pair_send[off - 1, k] = acc[pl.ds(begin, rows_out), :].astype(jnp.bfloat16)
            pair_copy(off, k).start()

    def fin_copy(part, k, source_group):
        out = (gk_out, gv_out)[part]
        return pltpu.make_async_remote_copy(
            src_ref=final.at[part, k],
            dst_ref=out.at[:, pl.ds(pl.multiple_of(source_group * HD, HD), HD)],
            send_sem=fin_ssem.at[part, k],
            recv_sem=fin_rsem.at[part, source_group],
            device_id=(ctx, k * repl + member),
            device_id_type=MESH,
        )

    for k in range(per_member):
        begin = pl.multiple_of((k * repl + member) * rows_out, rows_out)
        value = acc[pl.ds(begin, rows_out), :]
        for off in range(1, repl):
            pair_copy(off, k).wait_recv()
            value = value + pair_recv[off - 1, k].astype(jnp.float32)
        final[0, k] = value[:, :HD].astype(jnp.bfloat16)
        final[1, k] = value[:, HD:].astype(jnp.bfloat16)

        @pl.when(group != k)
        def _():
            fin_copy(0, k, group).start()
            fin_copy(1, k, group).start()

        @pl.when(group == k)
        def _():
            gk_out[:, pl.ds(gcol, HD)] = final[0, k]
            gv_out[:, pl.ds(gcol, HD)] = final[1, k]

    for level in range(levels):

        @pl.when(ctx + 2**level < n_ctx)
        def _():
            kv_copy(level).wait_send()

        @pl.when(ctx >= 2**level)
        def _():
            ret_copy(level).wait_send()

    for k in range(per_member):
        for off in range(1, repl):
            pair_copy(off, k).wait_send()
    for other in range(n_head):

        @pl.when(head != other)
        def _():
            dq_copy(other, other).wait_send()
            dq_copy(other, other).wait_recv()

    for k in range(kv_heads):

        @pl.when(group != k)
        def _():
            for part in range(2):
                fin_copy(part, k, k).wait_send()
                fin_copy(part, k, k).wait_recv()


def on_device(queries, keys, values, grad_out, block_index):
    shard_rows, q_width = queries.shape
    n_ctx = lax.axis_size("ctx")
    n_head = lax.axis_size("head")
    local_heads = q_width // HD
    kv_heads = keys.shape[1] // HD
    levels = n_ctx.bit_length() - 1
    repl = n_head // kv_heads
    rows_out = shard_rows // n_head
    tiles = shard_rows // BLK
    cols = local_heads * BLK
    pairs = tiles * (tiles + 1) // 2
    sizes = (n_ctx, n_head, kv_heads, local_heads, shard_rows, levels)
    bf16, f32 = jnp.bfloat16, jnp.float32
    vmem = pl.BlockSpec(memory_space=pltpu.VMEM)
    sem = pltpu.SemaphoreType.DMA
    elements = cols * BLK * (pairs + tiles * levels)
    return pl.pallas_call(
        functools.partial(kernel, sizes),
        out_shape=(
            jax.ShapeDtypeStruct((rows_out, n_head * q_width), bf16),
            jax.ShapeDtypeStruct((rows_out, kv_heads * HD), bf16),
            jax.ShapeDtypeStruct((rows_out, kv_heads * HD), bf16),
        ),
        in_specs=[vmem] * 4 + [pl.BlockSpec(memory_space=pltpu.SMEM)],
        out_specs=(vmem,) * 3,
        scratch_shapes=[
            pltpu.VMEM((shard_rows, 2 * HD), bf16),
            pltpu.VMEM((HD, shard_rows), bf16),
            pltpu.VMEM((HD, levels * BLK), bf16),
            pltpu.VMEM((levels, BLK, 2 * HD), bf16),
            pltpu.VMEM((levels, BLK, 2 * HD), bf16),
            pltpu.VMEM((pairs, BLK, cols), f32),
            pltpu.VMEM((pairs, BLK, cols), f32),
            pltpu.VMEM((levels, BLK, cols), f32),
            pltpu.VMEM((levels, BLK, cols), f32),
            pltpu.VMEM((tiles, HD, cols), f32),
            pltpu.VMEM((shard_rows, 2 * HD), f32),
            pltpu.VMEM((levels, BLK, 2 * HD), f32),
            pltpu.VMEM((levels, BLK, 2 * HD), bf16),
            pltpu.VMEM((levels, BLK, 2 * HD), bf16),
            pltpu.VMEM((shard_rows, q_width), bf16),
            pltpu.VMEM((max(repl - 1, 1), kv_heads, rows_out, 2 * HD), bf16),
            pltpu.VMEM((max(repl - 1, 1), kv_heads, rows_out, 2 * HD), bf16),
            pltpu.VMEM((2, kv_heads, rows_out, HD), bf16),
            sem((levels,)),
            sem((levels,)),
            sem((levels,)),
            sem((levels,)),
            sem((n_head,)),
            sem((n_head,)),
            sem((max(repl - 1, 1), kv_heads)),
            sem((max(repl - 1, 1), kv_heads)),
            sem((2, kv_heads)),
            sem((2, kv_heads)),
        ],
        compiler_params=pltpu.CompilerParams(
            collective_id=0, has_side_effects=True, vmem_limit_bytes=48 * 2**20
        ),
        cost_estimate=pl.CostEstimate(
            flops=10 * elements * HD, bytes_accessed=4 * 2**20, transcendentals=elements
        ),
    )(queries, grad_out, keys, values, block_index)


def solution(mesh):
    placed = (P("ctx", "head"), P("ctx", None), P("ctx", None), P("ctx", "head"), P())
    return jax.shard_map(
        on_device,
        mesh=mesh,
        in_specs=placed,
        out_specs=(P(("ctx", "head"), None), P(("ctx", "head"), None), P(("ctx", "head"), None)),
        check_vma=False,
    )
```

time: 82 us -> 48.8 us (0.60)
  Pallas kernels: 0 us -> 40.6 us
  waiting for transfers between devices: 27.8 us -> 0 us
  starting transfers between devices: 20.2 us -> 0 us
  matrix products: 15.8 us -> 0 us
  other arithmetic: 8.57 us -> 0 us
  between operations: 2.98 us -> 0.64 us
  local copies, waits for them, and re-layouts: 5.75 us -> 7.03 us
    pallas_call x0 -> x1, Pallas kernels: none -> 40.6 us  [on_device(): pl.pallas_call(functools.partial(kernel, sizes), out_shape=(jax.ShapeDtyp...]
    all_to_all x2 -> x0, waiting for transfers between devices: 18.3 us -> none  [the longest x1 13.1 us: on_device(): lax.all_to_all(owned.astype(jnp.bfloat16), 'head', split_axis=0, concat_a...]
    dot_general x20 -> x0, matrix products: 15.8 us -> none  [the longest x4 3.57 us: attend(): jnp.einsum('qd,kd->qk', grad_rows, value_all, preferred_element_type=jnp....]
    ppermute x6 -> x0, starting transfers between devices: 11.9 us -> none  [from_behind(): lax.ppermute(value, axis, [(source, source + steps) for source in range(l...]
    ppermute x6 -> x0, waiting for transfers between devices: 9.47 us -> none  [from_behind(): lax.ppermute(value, axis, [(source, source + steps) for source in range(l...]
    all_to_all x2 -> x0, starting transfers between devices: 8.33 us -> none  [the longest x1 4.87 us: on_device(): lax.all_to_all(dq_local, 'head', split_axis=0, concat_axis=1, tiled=True)]
    unnamed x4 -> x12, local copies, waits for them, and re-layouts: 0.01 us -> 7.03 us
    convert_element_type x6 -> x0, other arithmetic: 4.33 us -> none  [the longest x4 4.17 us: attend(): scores_low = (probs * (grad_probs - delta)).astype(jnp.bfloat16)]
  transfers between devices with their start and end apart: 8 -> 0, of which waited for: 6 -> 0; matrix products, arithmetic and copies ran while one was open for 3% -> 0% of each run, Pallas kernels for 0% -> 0%
where the time goes in v1:
time: 48.8 us; the launch traced here: 48.3 us
  Pallas kernels  40.6 us (83%)
  local copies, waits for them, and re-layouts  7.03 us (14%)
  between operations  0.64 us (1%)
    pallas_call x1, Pallas kernels, on_device(): pl.pallas_call(functools.partial(kernel, sizes), out_shape=(jax.ShapeDtyp...  40.6 us
    unnamed x12, local copies, waits for them, and re-layouts  7.03 us

profile of v1, /device:TPU:4, one launch (start us, length us, event | category | flops | bytes accessed | tf_op | source)
XLA Modules:
  0.0 48.3 jit_solution(13603352301482482642)
XLA Ops:
  0.6 0.8 %copy.8.index_ref = s32[8,3]{1,0:T(8,128)S(1)} copy(s32[8,3]{0,1:T(4,128)} %param.9) | data formatting | bytes 192 | tf_op args[4]
  1.4 0.0 copy-start
  1.4 1.0 %copy-done = bf16[1024,256]{1,0:T(8,128)(2,1)S(1)} copy-done((bf16[1024,256]{1,0:T(8,128)(2,1)S(1)}, bf16[1024,256]{1,0:T(8,128)(2,1)}, u32[]{:S(2)}) %copy-start) | copy-done | bytes 524312
  2.4 0.0 copy-start.1
  2.4 1.0 %copy-done.1 = bf16[1024,256]{1,0:T(8,128)(2,1)S(1)} copy-done((bf16[1024,256]{1,0:T(8,128)(2,1)S(1)}, bf16[1024,256]{1,0:T(8,128)(2,1)}, u32[]{:S(2)}) %copy-start.1) | copy-done | bytes 524312
  3.5 0.0 copy-start.2
  3.5 1.0 %copy-done.2 = bf16[1024,256]{1,0:T(8,128)(2,1)S(1)} copy-done((bf16[1024,256]{1,0:T(8,128)(2,1)S(1)}, bf16[1024,256]{1,0:T(8,128)(2,1)}, u32[]{:S(2)}) %copy-start.2) | copy-done | bytes 524312
  4.5 0.0 copy-start.3
  4.5 1.0 %copy-done.3 = bf16[1024,256]{1,0:T(8,128)(2,1)S(1)} copy-done((bf16[1024,256]{1,0:T(8,128)(2,1)S(1)}, bf16[1024,256]{1,0:T(8,128)(2,1)}, u32[]{:S(2)}) %copy-start.3) | copy-done | bytes 524312
  5.6 40.6 %shard_map.76 = (bf16[256,1024]{1,0:T(8,128)(2,1)S(1)}, bf16[256,256]{1,0:T(8,128)(2,1)S(1)}, bf16[256,256]{1,0:T(8,128)(2,1)S(1)}) custom-call(bf16[1024,256]{1,0:T(8,128)(2,1)S(1)} %copy-done, bf16[1024,256]{1,0:T(8,128)(2,1)S(1)} %copy-done.1, bf16[1024,256]{1,0:T(8,128)(2,1)S(1)} %copy-done.2, bf16[1024,256]{1,0:T(8,128)(2,1)S(1)} %copy-done.3, ...), custom_call_target="tpu_custom_call" | custom-call | flops 3690987520 | bytes 4194304 | tf_op jit(solution)/shard_map/pallas_call | solution.py:392
  46.2 0.8 %copy.12 = bf16[256,1024]{1,0:T(8,128)(2,1)} copy(bf16[256,1024]{1,0:T(8,128)(2,1)S(1)} %get-tuple-element.6) | data formatting | bytes 1048576
  47.0 0.7 %copy.13 = bf16[256,256]{1,0:T(8,128)(2,1)} copy(bf16[256,256]{1,0:T(8,128)(2,1)S(1)} %get-tuple-element.7) | data formatting | bytes 262144
  47.6 0.7 %copy.14 = bf16[256,256]{1,0:T(8,128)(2,1)} copy(bf16[256,256]{1,0:T(8,128)(2,1)S(1)} %get-tuple-element.8) | data formatting | bytes 262144
Async XLA Ops:
  1.4 1.0 %copy-start = (bf16[1024,256]{1,0:T(8,128)(2,1)S(1)}, bf16[1024,256]{1,0:T(8,128)(2,1)}, u32[]{:S(2)}) copy-start(bf16[1024,256]{1,0:T(8,128)(2,1)} %q_ref.1) | copy-start | bytes 1572868
  2.4 1.0 %copy-start.1 = (bf16[1024,256]{1,0:T(8,128)(2,1)S(1)}, bf16[1024,256]{1,0:T(8,128)(2,1)}, u32[]{:S(2)}) copy-start(bf16[1024,256]{1,0:T(8,128)(2,1)} %do_ref.1) | copy-start | bytes 1572868
  3.5 1.0 %copy-start.2 = (bf16[1024,256]{1,0:T(8,128)(2,1)S(1)}, bf16[1024,256]{1,0:T(8,128)(2,1)}, u32[]{:S(2)}) copy-start(bf16[1024,256]{1,0:T(8,128)(2,1)} %k_ref.1) | copy-start | bytes 1572868
  4.5 1.0 %copy-start.3 = (bf16[1024,256]{1,0:T(8,128)(2,1)S(1)}, bf16[1024,256]{1,0:T(8,128)(2,1)}, u32[]{:S(2)}) copy-start(bf16[1024,256]{1,0:T(8,128)(2,1)} %v_ref.1) | copy-start | bytes 1572868

commit v2 on v1

--- a/solution.py
+++ b/solution.py
@@ -9,6 +9,7 @@
 
 HD = 128
 BLK = 256
+VMEM_LIMIT = 60 * 2**20
 LOG2E = 1.4426950408889634
 MESH = pl.DeviceIdType.MESH
 NT = (((1,), (1,)), ((), ()))
@@ -21,14 +22,18 @@
 
 def kernel(
     sizes,
-    q_ref,
-    do_ref,
-    k_ref,
-    v_ref,
-    index_ref,
+    q_hbm,
+    do_hbm,
+    k_hbm,
+    v_hbm,
+    index_hbm,
     dq_out,
     gk_out,
     gv_out,
+    q_ref,
+    do_ref,
+    index_ref,
+    in_sem,
     own_kv,
     own_kt,
     part_kt,
@@ -73,6 +78,21 @@
     member = head % repl
     gcol = pl.multiple_of(group * HD, HD)
 
+    loads = [
+        pltpu.make_async_copy(src, dst, in_sem.at[number])
+        for number, (src, dst) in enumerate(
+            (
+                (k_hbm.at[:, pl.ds(gcol, HD)], own_kv.at[:, :HD]),
+                (v_hbm.at[:, pl.ds(gcol, HD)], own_kv.at[:, HD:]),
+                (index_hbm, index_ref),
+                (q_hbm, q_ref),
+                (do_hbm, do_ref),
+            )
+        )
+    ]
+    for load in loads:
+        load.start()
+
     barrier = pltpu.get_barrier_semaphore()
     greet = n_head - 1
     for level in range(levels):
@@ -92,8 +112,8 @@
             barrier, inc=1, device_id=(ctx, (head + off) % n_head), device_id_type=MESH
         )
 
-    own_kv[:, :HD] = k_ref[:, pl.ds(gcol, HD)]
-    own_kv[:, HD:] = v_ref[:, pl.ds(gcol, HD)]
+    for load in loads[:3]:
+        load.wait()
     blocks = []
 
     def is_block(level, block):
@@ -101,7 +121,7 @@
 
     for level in range(levels):
         target = jnp.minimum(ctx + 2**level, n_ctx - 1)
-        blocks.append(index_ref[target, level])
+        blocks.append(index_ref[level, target])
         chosen = jnp.zeros((BLK, 2 * HD), jnp.float32)
         for block in range(tiles):
             piece = own_kv[block * BLK : (block + 1) * BLK, :].astype(jnp.float32)
@@ -143,9 +163,14 @@
     def slot(tile, block):
         return tile * (tile + 1) // 2 + block
 
-    order = list(reversed(range(tiles)))
+    order = []
+    for tile in range((tiles + 1) // 2):
+        order += [tiles - 1 - tile] + ([tile] if tile != tiles - 1 - tile else [])
+    early = len(order) // 2
     key_pos = lax.broadcasted_iota(jnp.int32, (BLK, cols), 0)
     query_pos = lax.broadcasted_iota(jnp.int32, (BLK, cols), 1) % BLK
+    for load in loads[3:]:
+        load.wait()
     for block in range(tiles):
         rows = pl.ds(block * BLK, BLK)
         own_kt[:, rows] = own_kv[rows, :HD].T
@@ -185,7 +210,8 @@
         dead.append(jnp.where(ctx >= 2**level, 0.0, 1e30).astype(jnp.float32))
 
     final_stats = {}
-    for tile in order:
+
+    def partner_part(tile):
         q_cat, do_cat = stacked(q_ref, tile), stacked(do_ref, tile)
         top_own, total_own, mixed_own = own_stats[tile]
         top = top_own
@@ -222,6 +248,14 @@
             dq_t = piece if dq_t is None else dq_t + piece
         dq_part[tile] = dq_t
 
+    def send_partner():
+        for level in reversed(range(levels)):
+            ret_send[level] = acc_part[level].astype(jnp.bfloat16)
+
+            @pl.when(ctx >= 2**level)
+            def _():
+                ret_copy(level).start()
+
     def ret_copy(level):
         return pltpu.make_async_remote_copy(
             src_ref=ret_send.at[level],
@@ -232,13 +266,6 @@
             device_id_type=MESH,
         )
 
-    for level in reversed(range(levels)):
-        ret_send[level] = acc_part[level].astype(jnp.bfloat16)
-
-        @pl.when(ctx >= 2**level)
-        def _():
-            ret_copy(level).start()
-
     def dq_copy(dest, source):
         return pltpu.make_async_remote_copy(
             src_ref=dq_stage.at[pl.ds(dest * rows_out, rows_out), :],
@@ -249,7 +276,14 @@
             device_id_type=MESH,
         )
 
-    for tile in order:
+    def dq_keep(dest):
+        return pltpu.make_async_copy(
+            dq_stage.at[pl.ds(dest * rows_out, rows_out), :],
+            dq_out.at[:, pl.ds(pl.multiple_of(head * width, width), width)],
+            dq_ssem.at[dest],
+        )
+
+    def own_part(tile):
         q_cat, do_cat = stacked(q_ref, tile), stacked(do_ref, tile)
         inverse, delta = final_stats[tile]
         dq_t = dq_part[tile]
@@ -279,9 +313,16 @@
 
             @pl.when(head == dest)
             def _():
-                dq_out[:, pl.ds(pl.multiple_of(head * width, width), width)] = dq_stage[
-                    dest * rows_out : (dest + 1) * rows_out, :
-                ]
+                dq_keep(dest).start()
+
+    for tile in order[:early]:
+        partner_part(tile)
+        own_part(tile)
+    for tile in order[early:]:
+        partner_part(tile)
+    send_partner()
+    for tile in order[early:]:
+        own_part(tile)
 
     for level in range(levels):
 
@@ -324,6 +365,12 @@
             device_id_type=MESH,
         )
 
+    def fin_keep(part, k):
+        out = (gk_out, gv_out)[part]
+        return pltpu.make_async_copy(
+            final.at[part, k], out.at[:, pl.ds(gcol, HD)], fin_ssem.at[part, k]
+        )
+
     for k in range(per_member):
         begin = pl.multiple_of((k * repl + member) * rows_out, rows_out)
         value = acc[pl.ds(begin, rows_out), :]
@@ -340,8 +387,8 @@
 
         @pl.when(group == k)
         def _():
-            gk_out[:, pl.ds(gcol, HD)] = final[0, k]
-            gv_out[:, pl.ds(gcol, HD)] = final[1, k]
+            fin_keep(0, k).start()
+            fin_keep(1, k).start()
 
     for level in range(levels):
 
@@ -363,6 +410,10 @@
             dq_copy(other, other).wait_send()
             dq_copy(other, other).wait_recv()
 
+        @pl.when(head == other)
+        def _():
+            dq_keep(other).wait()
+
     for k in range(kv_heads):
 
         @pl.when(group != k)
@@ -370,6 +421,22 @@
             for part in range(2):
                 fin_copy(part, k, k).wait_send()
                 fin_copy(part, k, k).wait_recv()
+
+        @pl.when(group == k)
+        def _():
+            for part in range(2):
+                fin_keep(part, k).wait()
+
+
+def hand_over(a_in, b_in, c_in, a_out, b_out, c_out, sems):
+    copies = [
+        pltpu.make_async_copy(src, dst, sems.at[number])
+        for number, (src, dst) in enumerate(((a_in, a_out), (b_in, b_out), (c_in, c_out)))
+    ]
+    for copy in copies:
+        copy.start()
+    for copy in copies:
+        copy.wait()
 
 
 def on_device(queries, keys, values, grad_out, block_index):
@@ -386,19 +453,23 @@
     pairs = tiles * (tiles + 1) // 2
     sizes = (n_ctx, n_head, kv_heads, local_heads, shard_rows, levels)
     bf16, f32 = jnp.bfloat16, jnp.float32
-    vmem = pl.BlockSpec(memory_space=pltpu.VMEM)
+    hbm = pl.BlockSpec(memory_space=pltpu.HBM)
     sem = pltpu.SemaphoreType.DMA
     elements = cols * BLK * (pairs + tiles * levels)
-    return pl.pallas_call(
+    results = pl.pallas_call(
         functools.partial(kernel, sizes),
         out_shape=(
             jax.ShapeDtypeStruct((rows_out, n_head * q_width), bf16),
             jax.ShapeDtypeStruct((rows_out, kv_heads * HD), bf16),
             jax.ShapeDtypeStruct((rows_out, kv_heads * HD), bf16),
         ),
-        in_specs=[vmem] * 4 + [pl.BlockSpec(memory_space=pltpu.SMEM)],
-        out_specs=(vmem,) * 3,
+        in_specs=[hbm] * 5,
+        out_specs=(hbm,) * 3,
         scratch_shapes=[
+            pltpu.VMEM((shard_rows, q_width), bf16),
+            pltpu.VMEM((shard_rows, q_width), bf16),
+            pltpu.SMEM((levels, n_ctx), jnp.int32),
+            sem((5,)),
             pltpu.VMEM((shard_rows, 2 * HD), bf16),
             pltpu.VMEM((HD, shard_rows), bf16),
             pltpu.VMEM((HD, levels * BLK), bf16),
@@ -429,12 +500,20 @@
             sem((2, kv_heads)),
         ],
         compiler_params=pltpu.CompilerParams(
-            collective_id=0, has_side_effects=True, vmem_limit_bytes=48 * 2**20
+            collective_id=0, has_side_effects=True, vmem_limit_bytes=VMEM_LIMIT
         ),
         cost_estimate=pl.CostEstimate(
             flops=10 * elements * HD, bytes_accessed=4 * 2**20, transcendentals=elements
         ),
-    )(queries, grad_out, keys, values, block_index)
+    )(queries, grad_out, keys, values, block_index.T)
+    return pl.pallas_call(
+        hand_over,
+        out_shape=tuple(jax.ShapeDtypeStruct(x.shape, x.dtype) for x in results),
+        in_specs=[hbm] * 3,
+        out_specs=(hbm,) * 3,
+        scratch_shapes=[sem((3,))],
+        compiler_params=pltpu.CompilerParams(vmem_limit_bytes=VMEM_LIMIT),
+    )(*results)
 
 
 def solution(mesh):

time: 48.8 us -> 64.1 us (1.31); the launches traced: 48.3 us -> 62.9 us
  Pallas kernels: 40.6 us -> 62.2 us
  local copies, waits for them, and re-layouts: 7.03 us -> 0 us
    pallas_call x0 -> x1, Pallas kernels: none -> 25 us  [on_device(): pl.pallas_call(hand_over, out_shape=tuple((jax.ShapeDtypeStruct(x.shape,...]
    unnamed x12 -> x0, local copies, waits for them, and re-layouts: 7.03 us -> none
    pallas_call x1, Pallas kernels: 40.6 us -> 37.3 us  [on_device(): pl.pallas_call(functools.partial(kernel, sizes), out_shape=(jax.ShapeDtyp...]
where the time goes in v2:
time: 64.1 us; the launch traced here: 62.9 us
  Pallas kernels  62.2 us (97%)
    pallas_call x1, Pallas kernels, on_device(): pl.pallas_call(functools.partial(kernel, sizes), out_shape=(jax.ShapeDtyp...  37.3 us
    pallas_call x1, Pallas kernels, on_device(): pl.pallas_call(hand_over, out_shape=tuple((jax.ShapeDtypeStruct(x.shape,...  25 us

profile of v2, /device:TPU:4, one launch (start us, length us, event | category | flops | bytes accessed | tf_op | source)
XLA Modules:
  0.0 62.9 jit_solution(3449444895887221069)
XLA Ops:
  0.6 37.3 %shard_map.76 = (bf16[256,1024]{1,0:T(8,128)(2,1)}, bf16[256,256]{1,0:T(8,128)(2,1)}, bf16[256,256]{1,0:T(8,128)(2,1)}) custom-call(bf16[1024,256]{1,0:T(8,128)(2,1)} %q_hbm.1, bf16[1024,256]{1,0:T(8,128)(2,1)} %do_hbm.1, bf16[1024,256]{1,0:T(8,128)(2,1)} %k_hbm.1, bf16[1024,256]{1,0:T(8,128)(2,1)} %v_hbm.1, s32[3,8]{1,0:T(4,128)} %bitcast.1), custom_call_target="tpu_custom_call" | custom-call | flops 3690987520 | bytes 4194304 | tf_op jit(solution)/shard_map/pallas_call | solution.py:459
  37.9 25.0 %shard_map.77 = (bf16[256,1024]{1,0:T(8,128)(2,1)}, bf16[256,256]{1,0:T(8,128)(2,1)}, bf16[256,256]{1,0:T(8,128)(2,1)}) custom-call(bf16[256,1024]{1,0:T(8,128)(2,1)} %get-tuple-element.6.a_in, bf16[256,256]{1,0:T(8,128)(2,1)} %get-tuple-element.7.b_in, bf16[256,256]{1,0:T(8,128)(2,1)} %get-tuple-element.8.c_in), custom_call_target="tpu_custom_call" | custom-call | tf_op jit(solution)/shard_map/pallas_call | solution.py:509

commit v3 on v2

--- a/solution.py
+++ b/solution.py
@@ -12,12 +12,9 @@
 VMEM_LIMIT = 60 * 2**20
 LOG2E = 1.4426950408889634
 MESH = pl.DeviceIdType.MESH
-NT = (((1,), (1,)), ((), ()))
-NN = (((1,), (0,)), ((), ()))
-
-
-def dot(a, b, dims=NN):
-    return lax.dot_general(a, b, dims, preferred_element_type=jnp.float32)
+
+def dot(a, b):
+    return jnp.dot(a, b, preferred_element_type=jnp.float32)
 
 
 def kernel(
@@ -34,11 +31,14 @@
     do_ref,
     index_ref,
     in_sem,
+    q_t,
+    do_t,
     own_kv,
     own_kt,
     part_kt,
     kv_send,
     kv_recv,
+    s_tile,
     w_own,
     dp_own,
     w_part,
@@ -177,22 +177,25 @@
 
     own_stats = {}
     for tile in order:
+        q_t[tile] = stacked(q_ref, tile).T
+        do_t[tile] = stacked(do_ref, tile).T
+    for tile in order:
         q_cat, do_cat = stacked(q_ref, tile), stacked(do_ref, tile)
         top = None
         for block in range(tile + 1):
-            s = dot(own_kv[block * BLK : (block + 1) * BLK, :HD], q_cat, NT)
+            s = dot(own_kv[block * BLK : (block + 1) * BLK, :HD], q_t[tile])
             if block == tile:
                 s = jnp.where(key_pos <= query_pos, s, -1e30)
-            w_own[slot(tile, block)] = s
+            s_tile[block] = s
             high = jnp.max(s, axis=0, keepdims=True)
             top = high if top is None else jnp.maximum(top, high)
         top = top * c2
         total = jnp.zeros((1, cols), jnp.float32)
         mixed = jnp.zeros((1, cols), jnp.float32)
         for block in range(tile + 1):
-            w = jnp.exp2(w_own[slot(tile, block)] * c2 - top)
-            dp = dot(own_kv[block * BLK : (block + 1) * BLK, HD:], do_cat, NT)
-            w_own[slot(tile, block)] = w
+            w = jnp.exp2(s_tile[block] * c2 - top)
+            dp = dot(own_kv[block * BLK : (block + 1) * BLK, HD:], do_t[tile])
+            w_own[slot(tile, block)] = w.astype(jnp.bfloat16)
             dp_own[slot(tile, block)] = dp
             total = total + jnp.sum(w, axis=0, keepdims=True)
             mixed = mixed + jnp.sum(w * dp, axis=0, keepdims=True)
@@ -216,28 +219,29 @@
         top_own, total_own, mixed_own = own_stats[tile]
         top = top_own
         for level in range(levels):
-            s = dot(kv_recv[level, :, :HD], q_cat, NT)
-            w_part[level] = s
+            s = dot(kv_recv[level, :, :HD], q_t[tile])
+            s_tile[level] = s
             top = jnp.maximum(top, jnp.max(s, axis=0, keepdims=True) * c2 - dead[level])
         keep = jnp.exp2(top_own - top)
         total = total_own * keep
         mixed = mixed_own * keep
         for level in range(levels):
-            w = jnp.exp2(w_part[level] * c2 - (top + dead[level]))
-            dp = dot(kv_recv[level, :, HD:], do_cat, NT)
-            w_part[level] = w
+            w = jnp.exp2(s_tile[level] * c2 - (top + dead[level]))
+            dp = dot(kv_recv[level, :, HD:], do_t[tile])
+            w_part[level] = w.astype(jnp.bfloat16)
             dp_part[level] = dp
             total = total + jnp.sum(w, axis=0, keepdims=True)
             mixed = mixed + jnp.sum(w * dp, axis=0, keepdims=True)
         inverse = 1.0 / total
         delta = mixed * inverse
-        final_stats[tile] = (keep * inverse, delta)
+        inverse_low = inverse.astype(jnp.bfloat16)
+        final_stats[tile] = ((keep * inverse).astype(jnp.bfloat16), delta)
         dq_t = None
         for level in range(levels):
-            p = w_part[level] * inverse
-            ds = (p * (dp_part[level] - delta)).astype(jnp.bfloat16)
-            d_value = dot(p.astype(jnp.bfloat16), do_cat)
-            d_key = dot(ds, q_cat) * scale
+            p = w_part[level] * inverse_low
+            ds = p * (dp_part[level] - delta).astype(jnp.bfloat16)
+            d_value = dot(p, do_cat)
+            d_key = dot(ds, q_cat)
             if tile == order[0]:
                 acc_part[level, :, :HD] = d_key
                 acc_part[level, :, HD:] = d_value
@@ -250,7 +254,8 @@
 
     def send_partner():
         for level in reversed(range(levels)):
-            ret_send[level] = acc_part[level].astype(jnp.bfloat16)
+            ret_send[level, :, :HD] = (acc_part[level, :, :HD] * scale).astype(jnp.bfloat16)
+            ret_send[level, :, HD:] = acc_part[level, :, HD:].astype(jnp.bfloat16)
 
             @pl.when(ctx >= 2**level)
             def _():
@@ -285,13 +290,13 @@
 
     def own_part(tile):
         q_cat, do_cat = stacked(q_ref, tile), stacked(do_ref, tile)
-        inverse, delta = final_stats[tile]
+        inverse_low, delta = final_stats[tile]
         dq_t = dq_part[tile]
         for block in range(tile + 1):
-            p = w_own[slot(tile, block)] * inverse
-            ds = (p * (dp_own[slot(tile, block)] - delta)).astype(jnp.bfloat16)
-            d_value = dot(p.astype(jnp.bfloat16), do_cat)
-            d_key = dot(ds, q_cat) * scale
+            p = w_own[slot(tile, block)] * inverse_low
+            ds = p * (dp_own[slot(tile, block)] - delta).astype(jnp.bfloat16)
+            d_value = dot(p, do_cat)
+            d_key = dot(ds, q_cat)
             rows = slice(block * BLK, (block + 1) * BLK)
             if tile == order[0]:
                 acc[rows, :HD] = d_key
@@ -332,7 +337,7 @@
 
     for block in range(tiles):
         rows = slice(block * BLK, (block + 1) * BLK)
-        value = acc[rows, :]
+        value = jnp.concatenate([acc[rows, :HD] * scale, acc[rows, HD:]], axis=1)
         for level in range(levels):
             back = ret_recv[level].astype(jnp.float32)
             value = value + back * is_block(level, block)
@@ -428,15 +433,23 @@
                 fin_keep(part, k).wait()
 
 
-def hand_over(a_in, b_in, c_in, a_out, b_out, c_out, sems):
-    copies = [
-        pltpu.make_async_copy(src, dst, sems.at[number])
-        for number, (src, dst) in enumerate(((a_in, a_out), (b_in, b_out), (c_in, c_out)))
+def hand_over(a_in, b_in, c_in, a_out, b_out, c_out, a_mid, b_mid, c_mid, in_sems, out_sems):
+    mids = (a_mid, b_mid, c_mid)
+    loads = [
+        pltpu.make_async_copy(src, dst, in_sems.at[number])
+        for number, (src, dst) in enumerate(zip((a_in, b_in, c_in), mids))
     ]
-    for copy in copies:
-        copy.start()
-    for copy in copies:
-        copy.wait()
+    stores = [
+        pltpu.make_async_copy(src, dst, out_sems.at[number])
+        for number, (src, dst) in enumerate(zip(mids, (a_out, b_out, c_out)))
+    ]
+    for load in loads:
+        load.start()
+    for load, store in zip(loads, stores):
+        load.wait()
+        store.start()
+    for store in stores:
+        store.wait()
 
 
 def on_device(queries, keys, values, grad_out, block_index):
@@ -470,14 +483,17 @@
             pltpu.VMEM((shard_rows, q_width), bf16),
             pltpu.SMEM((levels, n_ctx), jnp.int32),
             sem((5,)),
+            pltpu.VMEM((tiles, HD, cols), bf16),
+            pltpu.VMEM((tiles, HD, cols), bf16),
             pltpu.VMEM((shard_rows, 2 * HD), bf16),
             pltpu.VMEM((HD, shard_rows), bf16),
             pltpu.VMEM((HD, levels * BLK), bf16),
             pltpu.VMEM((levels, BLK, 2 * HD), bf16),
             pltpu.VMEM((levels, BLK, 2 * HD), bf16),
+            pltpu.VMEM((max(tiles, levels), BLK, cols), f32),
+            pltpu.VMEM((pairs, BLK, cols), bf16),
             pltpu.VMEM((pairs, BLK, cols), f32),
-            pltpu.VMEM((pairs, BLK, cols), f32),
-            pltpu.VMEM((levels, BLK, cols), f32),
+            pltpu.VMEM((levels, BLK, cols), bf16),
             pltpu.VMEM((levels, BLK, cols), f32),
             pltpu.VMEM((tiles, HD, cols), f32),
             pltpu.VMEM((shard_rows, 2 * HD), f32),
@@ -511,7 +527,7 @@
         out_shape=tuple(jax.ShapeDtypeStruct(x.shape, x.dtype) for x in results),
         in_specs=[hbm] * 3,
         out_specs=(hbm,) * 3,
-        scratch_shapes=[sem((3,))],
+        scratch_shapes=[pltpu.VMEM(x.shape, x.dtype) for x in results] + [sem((3,)), sem((3,))],
         compiler_params=pltpu.CompilerParams(vmem_limit_bytes=VMEM_LIMIT),
     )(*results)
 

time: 64.1 us -> 41 us (0.64)
  the two profiles are of different devices: /device:TPU:4 before, /device:TPU:27 now
where the time goes in v3:
time: 41 us; the launch traced here: 40.8 us
  Pallas kernels  40.2 us (98%)
  between operations  0.64 us (2%)
    pallas_call x1, Pallas kernels, on_device(): pl.pallas_call(functools.partial(kernel, sizes), out_shape=(jax.ShapeDtyp...  38.2 us
    pallas_call x1, Pallas kernels, on_device(): pl.pallas_call(hand_over, out_shape=tuple((jax.ShapeDtypeStruct(x.shape,...  1.96 us

profile of v3, /device:TPU:27, one launch (start us, length us, event | category | flops | bytes accessed | tf_op | source)
XLA Modules:
  0.0 40.8 jit_solution(3026732432193115499)
XLA Ops:
  0.6 38.2 %shard_map.76 = (bf16[256,1024]{1,0:T(8,128)(2,1)}, bf16[256,256]{1,0:T(8,128)(2,1)}, bf16[256,256]{1,0:T(8,128)(2,1)}) custom-call(bf16[1024,256]{1,0:T(8,128)(2,1)} %q_hbm.1, bf16[1024,256]{1,0:T(8,128)(2,1)} %do_hbm.1, bf16[1024,256]{1,0:T(8,128)(2,1)} %k_hbm.1, bf16[1024,256]{1,0:T(8,128)(2,1)} %v_hbm.1, s32[3,8]{1,0:T(4,128)} %bitcast.1), custom_call_target="tpu_custom_call" | custom-call | flops 3690987520 | bytes 4194304 | tf_op jit(solution)/shard_map/pallas_call | solution.py:472
  38.8 2.0 %shard_map.77 = (bf16[256,1024]{1,0:T(8,128)(2,1)}, bf16[256,256]{1,0:T(8,128)(2,1)}, bf16[256,256]{1,0:T(8,128)(2,1)}) custom-call(bf16[256,1024]{1,0:T(8,128)(2,1)} %get-tuple-element.6.a_in, bf16[256,256]{1,0:T(8,128)(2,1)} %get-tuple-element.7.b_in, bf16[256,256]{1,0:T(8,128)(2,1)} %get-tuple-element.8.c_in), custom_call_target="tpu_custom_call" | custom-call | tf_op jit(solution)/shard_map/pallas_call | solution.py:525

commit v4 on v3

--- a/solution.py
+++ b/solution.py
@@ -49,8 +49,10 @@
     ret_send,
     ret_recv,
     dq_stage,
-    pair_send,
-    pair_recv,
+    part_send,
+    part_recv,
+    own_send,
+    own_recv,
     final,
     kv_ssem,
     kv_rsem,
@@ -58,14 +60,15 @@
     ret_rsem,
     dq_ssem,
     dq_rsem,
-    pair_ssem,
-    pair_rsem,
+    part_ssem,
+    part_rsem,
+    own_ssem,
+    own_rsem,
     fin_ssem,
     fin_rsem,
 ):
     n_ctx, n_head, kv_heads, local_heads, shard_rows, levels = sizes
     repl = n_head // kv_heads
-    per_member = n_head // repl
     rows_out = shard_rows // n_head
     tiles = shard_rows // BLK
     cols = local_heads * BLK
@@ -77,6 +80,9 @@
     group = head // repl
     member = head % repl
     gcol = pl.multiple_of(group * HD, HD)
+    mate = group * repl + (1 - member)
+    mcol = pl.multiple_of(member * HD, HD)
+    ocol = pl.multiple_of((1 - member) * HD, HD)
 
     loads = [
         pltpu.make_async_copy(src, dst, in_sem.at[number])
@@ -152,7 +158,7 @@
 
         @pl.when(ctx + 2**level >= n_ctx)
         def _():
-            ret_recv[level] = jnp.zeros((BLK, 2 * HD), jnp.bfloat16)
+            ret_recv[level] = jnp.zeros((BLK, HD), jnp.bfloat16)
 
     def stacked(ref, tile):
         rows = pl.ds(tile * BLK, BLK)
@@ -252,14 +258,49 @@
             dq_t = piece if dq_t is None else dq_t + piece
         dq_part[tile] = dq_t
 
+    def part_copy(level):
+        return pltpu.make_async_remote_copy(
+            src_ref=part_send.at[level],
+            dst_ref=part_recv.at[level],
+            send_sem=part_ssem.at[level],
+            recv_sem=part_rsem.at[level],
+            device_id=(ctx, mate),
+            device_id_type=MESH,
+        )
+
+    def own_copy(block):
+        return pltpu.make_async_remote_copy(
+            src_ref=own_send.at[block],
+            dst_ref=own_recv.at[block],
+            send_sem=own_ssem.at[block],
+            recv_sem=own_rsem.at[block],
+            device_id=(ctx, mate),
+            device_id_type=MESH,
+        )
+
     def send_partner():
         for level in reversed(range(levels)):
-            ret_send[level, :, :HD] = (acc_part[level, :, :HD] * scale).astype(jnp.bfloat16)
-            ret_send[level, :, HD:] = acc_part[level, :, HD:].astype(jnp.bfloat16)
 
             @pl.when(ctx >= 2**level)
             def _():
+                part_send[level] = acc_part[level, :, pl.ds(ocol, HD)].astype(jnp.bfloat16)
+                part_copy(level).start()
+
+    def return_partner():
+        for level in reversed(range(levels)):
+
+            @pl.when(ctx >= 2**level)
+            def _():
+                part_copy(level).wait_recv()
+                ret_send[level] = (
+                    acc_part[level, :, pl.ds(mcol, HD)] + part_recv[level].astype(jnp.float32)
+                ).astype(jnp.bfloat16)
                 ret_copy(level).start()
+
+    def send_own(block):
+        rows = slice(block * BLK, (block + 1) * BLK)
+        own_send[block] = acc[rows, pl.ds(ocol, HD)].astype(jnp.bfloat16)
+        own_copy(block).start()
 
     def ret_copy(level):
         return pltpu.make_async_remote_copy(
@@ -320,14 +361,17 @@
             def _():
                 dq_keep(dest).start()
 
-    for tile in order[:early]:
-        partner_part(tile)
-        own_part(tile)
-    for tile in order[early:]:
+    last_use = [max(order.index(tile) for tile in range(block, tiles)) for block in range(tiles)]
+    for tile in order:
         partner_part(tile)
     send_partner()
-    for tile in order[early:]:
+    for number, tile in enumerate(order):
         own_part(tile)
+        for block in reversed(range(tiles)):
+            if last_use[block] == number:
+                send_own(block)
+        if number == early - 1:
+            return_partner()
 
     for level in range(levels):
 
@@ -335,65 +379,44 @@
         def _():
             ret_copy(level).wait_recv()
 
-    for block in range(tiles):
-        rows = slice(block * BLK, (block + 1) * BLK)
-        value = jnp.concatenate([acc[rows, :HD] * scale, acc[rows, HD:]], axis=1)
-        for level in range(levels):
-            back = ret_recv[level].astype(jnp.float32)
-            value = value + back * is_block(level, block)
-        acc[rows, :] = value
-
-    def pair_copy(off, k):
-        return pltpu.make_async_remote_copy(
-            src_ref=pair_send.at[off - 1, k],
-            dst_ref=pair_recv.at[off - 1, k],
-            send_sem=pair_ssem.at[off - 1, k],
-            recv_sem=pair_rsem.at[off - 1, k],
-            device_id=(ctx, group * repl + (member + off) % repl),
-            device_id_type=MESH,
-        )
-
-    for k in range(per_member):
-        for off in range(1, repl):
-            begin = pl.multiple_of((k * repl + (member + off) % repl) * rows_out, rows_out)
-            pair_send[off - 1, k] = acc[pl.ds(begin, rows_out), :].astype(jnp.bfloat16)
-            pair_copy(off, k).start()
-
-    def fin_copy(part, k, source_group):
+    factor = jnp.where(member == 0, scale, 1.0).astype(jnp.float32)
+
+    def fin_copy(part, dest, source):
         out = (gk_out, gv_out)[part]
         return pltpu.make_async_remote_copy(
-            src_ref=final.at[part, k],
-            dst_ref=out.at[:, pl.ds(pl.multiple_of(source_group * HD, HD), HD)],
-            send_sem=fin_ssem.at[part, k],
-            recv_sem=fin_rsem.at[part, source_group],
-            device_id=(ctx, k * repl + member),
+            src_ref=final.at[pl.ds(dest * rows_out, rows_out), :],
+            dst_ref=out.at[:, pl.ds(pl.multiple_of(source // repl * HD, HD), HD)],
+            send_sem=fin_ssem.at[dest],
+            recv_sem=fin_rsem.at[source],
+            device_id=(ctx, dest),
             device_id_type=MESH,
         )
 
-    def fin_keep(part, k):
+    def fin_keep(part, dest):
         out = (gk_out, gv_out)[part]
         return pltpu.make_async_copy(
-            final.at[part, k], out.at[:, pl.ds(gcol, HD)], fin_ssem.at[part, k]
-        )
-
-    for k in range(per_member):
-        begin = pl.multiple_of((k * repl + member) * rows_out, rows_out)
-        value = acc[pl.ds(begin, rows_out), :]
-        for off in range(1, repl):
-            pair_copy(off, k).wait_recv()
-            value = value + pair_recv[off - 1, k].astype(jnp.float32)
-        final[0, k] = value[:, :HD].astype(jnp.bfloat16)
-        final[1, k] = value[:, HD:].astype(jnp.bfloat16)
-
-        @pl.when(group != k)
-        def _():
-            fin_copy(0, k, group).start()
-            fin_copy(1, k, group).start()
-
-        @pl.when(group == k)
-        def _():
-            fin_keep(0, k).start()
-            fin_keep(1, k).start()
+            final.at[pl.ds(dest * rows_out, rows_out), :],
+            out.at[:, pl.ds(gcol, HD)],
+            fin_ssem.at[dest],
+        )
+
+    for block in reversed(range(tiles)):
+        rows = slice(block * BLK, (block + 1) * BLK)
+        own_copy(block).wait_recv()
+        value = acc[rows, pl.ds(mcol, HD)] + own_recv[block].astype(jnp.float32)
+        for level in range(levels):
+            value = value + ret_recv[level].astype(jnp.float32) * is_block(level, block)
+        final[rows, :] = (value * factor).astype(jnp.bfloat16)
+        for dest in range(block * BLK // rows_out, (block + 1) * BLK // rows_out):
+            for part in range(2):
+
+                @pl.when((head != dest) & (member == part))
+                def _():
+                    fin_copy(part, dest, head).start()
+
+                @pl.when((head == dest) & (member == part))
+                def _():
+                    fin_keep(part, dest).start()
 
     for level in range(levels):
 
@@ -405,32 +428,27 @@
         def _():
             ret_copy(level).wait_send()
 
-    for k in range(per_member):
-        for off in range(1, repl):
-            pair_copy(off, k).wait_send()
+    for level in range(levels):
+
+        @pl.when(ctx >= 2**level)
+        def _():
+            part_copy(level).wait_send()
+
+    for block in range(tiles):
+        own_copy(block).wait_send()
     for other in range(n_head):
 
         @pl.when(head != other)
         def _():
             dq_copy(other, other).wait_send()
             dq_copy(other, other).wait_recv()
+            fin_copy(0, other, other).wait_send()
+            fin_copy(0, other, other).wait_recv()
 
         @pl.when(head == other)
         def _():
             dq_keep(other).wait()
-
-    for k in range(kv_heads):
-
-        @pl.when(group != k)
-        def _():
-            for part in range(2):
-                fin_copy(part, k, k).wait_send()
-                fin_copy(part, k, k).wait_recv()
-
-        @pl.when(group == k)
-        def _():
-            for part in range(2):
-                fin_keep(part, k).wait()
+            fin_keep(0, other).wait()
 
 
 def hand_over(a_in, b_in, c_in, a_out, b_out, c_out, a_mid, b_mid, c_mid, in_sems, out_sems):
@@ -459,7 +477,6 @@
     local_heads = q_width // HD
     kv_heads = keys.shape[1] // HD
     levels = n_ctx.bit_length() - 1
-    repl = n_head // kv_heads
     rows_out = shard_rows // n_head
     tiles = shard_rows // BLK
     cols = local_heads * BLK
@@ -498,22 +515,26 @@
             pltpu.VMEM((tiles, HD, cols), f32),
             pltpu.VMEM((shard_rows, 2 * HD), f32),
             pltpu.VMEM((levels, BLK, 2 * HD), f32),
-            pltpu.VMEM((levels, BLK, 2 * HD), bf16),
-            pltpu.VMEM((levels, BLK, 2 * HD), bf16),
+            pltpu.VMEM((levels, BLK, HD), bf16),
+            pltpu.VMEM((levels, BLK, HD), bf16),
             pltpu.VMEM((shard_rows, q_width), bf16),
-            pltpu.VMEM((max(repl - 1, 1), kv_heads, rows_out, 2 * HD), bf16),
-            pltpu.VMEM((max(repl - 1, 1), kv_heads, rows_out, 2 * HD), bf16),
-            pltpu.VMEM((2, kv_heads, rows_out, HD), bf16),
+            pltpu.VMEM((levels, BLK, HD), bf16),
+            pltpu.VMEM((levels, BLK, HD), bf16),
+            pltpu.VMEM((tiles, BLK, HD), bf16),
+            pltpu.VMEM((tiles, BLK, HD), bf16),
+            pltpu.VMEM((shard_rows, HD), bf16),
             sem((levels,)),
             sem((levels,)),
             sem((levels,)),
             sem((levels,)),
             sem((n_head,)),
             sem((n_head,)),
-            sem((max(repl - 1, 1), kv_heads)),
-            sem((max(repl - 1, 1), kv_heads)),
-            sem((2, kv_heads)),
-            sem((2, kv_heads)),
+            sem((levels,)),
+            sem((levels,)),
+            sem((tiles,)),
+            sem((tiles,)),
+            sem((n_head,)),
+            sem((n_head,)),
         ],
         compiler_params=pltpu.CompilerParams(
             collective_id=0, has_side_effects=True, vmem_limit_bytes=VMEM_LIMIT

time: 41 us -> 48.2 us (1.18)
  the two profiles are of different devices: /device:TPU:27 before, /device:TPU:4 now
where the time goes in v4:
time: 48.2 us; the launch traced here: 48 us
  Pallas kernels  47.4 us (98%)
  between operations  0.64 us (1%)
    pallas_call x1, Pallas kernels, on_device(): pl.pallas_call(functools.partial(kernel, sizes), out_shape=(jax.ShapeDtyp...  45.4 us
    pallas_call x1, Pallas kernels, on_device(): pl.pallas_call(hand_over, out_shape=tuple((jax.ShapeDtypeStruct(x.shape,...  1.96 us

profile of v4, /device:TPU:4, one launch (start us, length us, event | category | flops | bytes accessed | tf_op | source)
XLA Modules:
  0.0 48.0 jit_solution(2184499147686287787)
XLA Ops:
  0.6 45.4 %shard_map.76 = (bf16[256,1024]{1,0:T(8,128)(2,1)}, bf16[256,256]{1,0:T(8,128)(2,1)}, bf16[256,256]{1,0:T(8,128)(2,1)}) custom-call(bf16[1024,256]{1,0:T(8,128)(2,1)} %q_hbm.1, bf16[1024,256]{1,0:T(8,128)(2,1)} %do_hbm.1, bf16[1024,256]{1,0:T(8,128)(2,1)} %k_hbm.1, bf16[1024,256]{1,0:T(8,128)(2,1)} %v_hbm.1, s32[3,8]{1,0:T(4,128)} %bitcast.1), custom_call_target="tpu_custom_call" | custom-call | flops 3690987520 | bytes 4194304 | tf_op jit(solution)/shard_map/pallas_call | solution.py:489
  46.0 2.0 %shard_map.77 = (bf16[256,1024]{1,0:T(8,128)(2,1)}, bf16[256,256]{1,0:T(8,128)(2,1)}, bf16[256,256]{1,0:T(8,128)(2,1)}) custom-call(bf16[256,1024]{1,0:T(8,128)(2,1)} %get-tuple-element.6.a_in, bf16[256,256]{1,0:T(8,128)(2,1)} %get-tuple-element.7.b_in, bf16[256,256]{1,0:T(8,128)(2,1)} %get-tuple-element.8.c_in), custom_call_target="tpu_custom_call" | custom-call | tf_op jit(solution)/shard_map/pallas_call | solution.py:546

commit v5 on v4

--- a/solution.py
+++ b/solution.py
@@ -362,16 +362,22 @@
                 dq_keep(dest).start()
 
     last_use = [max(order.index(tile) for tile in range(block, tiles)) for block in range(tiles)]
-    for tile in order:
-        partner_part(tile)
-    send_partner()
-    for number, tile in enumerate(order):
-        own_part(tile)
+
+    def finish(number):
+        own_part(order[number])
         for block in reversed(range(tiles)):
             if last_use[block] == number:
                 send_own(block)
-        if number == early - 1:
-            return_partner()
+
+    for number in range(early):
+        partner_part(order[number])
+        finish(number)
+    for number in range(early, tiles):
+        partner_part(order[number])
+    send_partner()
+    for number in range(early, tiles):
+        finish(number)
+    return_partner()
 
     for level in range(levels):
 

time: 48.2 us -> 43.8 us (0.909)
  Pallas kernels: 47.4 us -> 43 us
    pallas_call x1, Pallas kernels: 45.4 us -> 41 us  [on_device(): pl.pallas_call(functools.partial(kernel, sizes), out_shape=(jax.ShapeDtyp...]
where the time goes in v5:
time: 43.8 us; the launch traced here: 43.6 us
  Pallas kernels  43 us (98%)
  between operations  0.64 us (1%)
    pallas_call x1, Pallas kernels, on_device(): pl.pallas_call(functools.partial(kernel, sizes), out_shape=(jax.ShapeDtyp...  41 us
    pallas_call x1, Pallas kernels, on_device(): pl.pallas_call(hand_over, out_shape=tuple((jax.ShapeDtypeStruct(x.shape,...  1.96 us

profile of v5, /device:TPU:4, one launch (start us, length us, event | category | flops | bytes accessed | tf_op | source)
XLA Modules:
  0.0 43.6 jit_solution(17621415966730078728)
XLA Ops:
  0.6 41.0 %shard_map.76 = (bf16[256,1024]{1,0:T(8,128)(2,1)}, bf16[256,256]{1,0:T(8,128)(2,1)}, bf16[256,256]{1,0:T(8,128)(2,1)}) custom-call(bf16[1024,256]{1,0:T(8,128)(2,1)} %q_hbm.1, bf16[1024,256]{1,0:T(8,128)(2,1)} %do_hbm.1, bf16[1024,256]{1,0:T(8,128)(2,1)} %k_hbm.1, bf16[1024,256]{1,0:T(8,128)(2,1)} %v_hbm.1, s32[3,8]{1,0:T(4,128)} %bitcast.1), custom_call_target="tpu_custom_call" | custom-call | flops 3690987520 | bytes 4194304 | tf_op jit(solution)/shard_map/pallas_call | solution.py:495
  41.7 2.0 %shard_map.77 = (bf16[256,1024]{1,0:T(8,128)(2,1)}, bf16[256,256]{1,0:T(8,128)(2,1)}, bf16[256,256]{1,0:T(8,128)(2,1)}) custom-call(bf16[256,1024]{1,0:T(8,128)(2,1)} %get-tuple-element.6.a_in, bf16[256,256]{1,0:T(8,128)(2,1)} %get-tuple-element.7.b_in, bf16[256,256]{1,0:T(8,128)(2,1)} %get-tuple-element.8.c_in), custom_call_target="tpu_custom_call" | custom-call | tf_op jit(solution)/shard_map/pallas_call | solution.py:552

commit v6 on v3

--- a/solution.py
+++ b/solution.py
@@ -54,6 +54,8 @@
     final,
     kv_ssem,
     kv_rsem,
+    relay_ssem,
+    relay_rsem,
     ret_ssem,
     ret_rsem,
     dq_ssem,
@@ -77,6 +79,9 @@
     group = head // repl
     member = head % repl
     gcol = pl.multiple_of(group * HD, HD)
+    half = BLK // repl
+    my_half = pl.multiple_of(member * half, half)
+    mate = group * repl + (member + 1) % repl
 
     loads = [
         pltpu.make_async_copy(src, dst, in_sem.at[number])
@@ -132,13 +137,31 @@
 
     def kv_copy(level):
         return pltpu.make_async_remote_copy(
-            src_ref=kv_send.at[level],
-            dst_ref=kv_recv.at[level],
+            src_ref=kv_send.at[level, pl.ds(my_half, half), :],
+            dst_ref=kv_recv.at[level, pl.ds(my_half, half), :],
             send_sem=kv_ssem.at[level],
             recv_sem=kv_rsem.at[level],
             device_id=(jnp.minimum(ctx + 2**level, n_ctx - 1), head),
             device_id_type=MESH,
         )
+
+    def kv_relay(level):
+        return pltpu.make_async_remote_copy(
+            src_ref=kv_recv.at[level, pl.ds(my_half, half), :],
+            dst_ref=kv_recv.at[level, pl.ds(my_half, half), :],
+            send_sem=relay_ssem.at[level],
+            recv_sem=relay_rsem.at[level],
+            device_id=(ctx, mate),
+            device_id_type=MESH,
+        )
+
+    def relay():
+        for level in reversed(range(levels)):
+
+            @pl.when(ctx >= 2**level)
+            def _():
+                kv_copy(level).wait_recv()
+                kv_relay(level).start()
 
     for level in reversed(range(levels)):
 
@@ -200,12 +223,14 @@
             total = total + jnp.sum(w, axis=0, keepdims=True)
             mixed = mixed + jnp.sum(w * dp, axis=0, keepdims=True)
         own_stats[tile] = (top, total, mixed)
+        if tile == order[early]:
+            relay()
 
     for level in range(levels):
 
         @pl.when(ctx >= 2**level)
         def _():
-            kv_copy(level).wait_recv()
+            kv_relay(level).wait_recv()
 
     dead = []
     for level in range(levels):
@@ -404,6 +429,7 @@
         @pl.when(ctx >= 2**level)
         def _():
             ret_copy(level).wait_send()
+            kv_relay(level).wait_send()
 
     for k in range(per_member):
         for off in range(1, repl):
@@ -508,6 +534,8 @@
             sem((levels,)),
             sem((levels,)),
             sem((levels,)),
+            sem((levels,)),
+            sem((levels,)),
             sem((n_head,)),
             sem((n_head,)),
             sem((max(repl - 1, 1), kv_heads)),

time: 41 us -> 42 us (1.024)
  the two profiles are of different devices: /device:TPU:27 before, /device:TPU:19 now
where the time goes in v6:
time: 42 us; the launch traced here: 41.8 us
  Pallas kernels  41.2 us (98%)
  between operations  0.64 us (2%)
    pallas_call x1, Pallas kernels, on_device(): pl.pallas_call(functools.partial(kernel, sizes), out_shape=(jax.ShapeDtyp...  39.2 us
    pallas_call x1, Pallas kernels, on_device(): pl.pallas_call(hand_over, out_shape=tuple((jax.ShapeDtypeStruct(x.shape,...  1.96 us

profile of v6, /device:TPU:19, one launch (start us, length us, event | category | flops | bytes accessed | tf_op | source)
XLA Modules:
  0.0 41.8 jit_solution(17470095645871943889)
XLA Ops:
  0.6 39.2 %shard_map.76 = (bf16[256,1024]{1,0:T(8,128)(2,1)}, bf16[256,256]{1,0:T(8,128)(2,1)}, bf16[256,256]{1,0:T(8,128)(2,1)}) custom-call(bf16[1024,256]{1,0:T(8,128)(2,1)} %q_hbm.1, bf16[1024,256]{1,0:T(8,128)(2,1)} %do_hbm.1, bf16[1024,256]{1,0:T(8,128)(2,1)} %k_hbm.1, bf16[1024,256]{1,0:T(8,128)(2,1)} %v_hbm.1, s32[3,8]{1,0:T(4,128)} %bitcast.1), custom_call_target="tpu_custom_call" | custom-call | flops 3690987520 | bytes 4194304 | tf_op jit(solution)/shard_map/pallas_call | solution.py:498
  39.8 2.0 %shard_map.77 = (bf16[256,1024]{1,0:T(8,128)(2,1)}, bf16[256,256]{1,0:T(8,128)(2,1)}, bf16[256,256]{1,0:T(8,128)(2,1)}) custom-call(bf16[256,1024]{1,0:T(8,128)(2,1)} %get-tuple-element.6.a_in, bf16[256,256]{1,0:T(8,128)(2,1)} %get-tuple-element.7.b_in, bf16[256,256]{1,0:T(8,128)(2,1)} %get-tuple-element.8.c_in), custom_call_target="tpu_custom_call" | custom-call | tf_op jit(solution)/shard_map/pallas_call | solution.py:553
